TPU v7x, 256 devices: a whole 4x4x8 slice. The times are simulated.
256 devices in a mesh: ctx: 16 (over y, x_hi, core), tp: 16 (over z, x_lo).
Axes of the slice: x: 4 (x_hi: 2, x_lo: 2; x = x_hi * 2 + x_lo), y: 4, z: 8, core: 2. Of those that a mesh axis runs over, the one named last changes fastest.
Arguments:
- stream: bfloat16 [6144, 8192], P('ctx', 'tp'), may hold values from -40 to 40
- pending: bfloat16 [16, 6144, 8192], P('tp', 'ctx'), may hold values from -5 to 5
- norm_gain: bfloat16 [8192], replicated, may hold values from 0.099609375 to 1.8984375
- w_query: bfloat16 [8192, 4096], P('ctx', 'tp'), may hold values from -0.0625 to 0.0625
- w_key: bfloat16 [8192, 1024], P('ctx'), may hold values from -0.375 to 0.375
- w_value: bfloat16 [8192, 1024], P('ctx'), may hold values from -0.1875 to 0.1875
- w_out: bfloat16 [4096, 8192], P('tp', 'ctx'), may hold values from -0.09375 to 0.09375
- prefix_keys: bfloat16 [8, 12288, 128], P(None, 'ctx'), may hold values from -600 to 600
- prefix_values: bfloat16 [8, 12288, 128], P(None, 'ctx'), may hold values from -6 to 6
- prefix_segments: int32 [12288], P('ctx'), may hold values from 0 to 15, never falling along the last dimension, each value on 1 to 1536 neighbouring positions
- stretch_segments: int32 [6144], P('ctx'), may hold values from 0 to 15, never falling along the last dimension, each value on 1 to 768 neighbouring positions
- stretch_offset: int32 [1], replicated, may hold values from 12288 to 24575
Outputs:
- output: bfloat16 [6144, 8192], P('ctx', 'tp')
Inputs may be any that keep to these rules, and one draw needn't show every extreme that they name: `prefix_segments`: never falls along the positions; every trajectory 0 to 15 occurs. `stretch_segments`: never falls along the positions; every trajectory 0 to 15 occurs.
All inputs are finite; a program needn't handle non-finite values.
Results may differ from a plain program's by a relative error of at most 0.024.
Values may be sent and summed in bfloat16 or wider, within the bound.
A program may use at most 256 MiB of HBM per device.

v0:
```python
import math

import jax
import jax.numpy as jnp
from jax import lax
from jax.sharding import PartitionSpec as P

HQ = 32
KVH = 8
HD = 128


ROPE_BASE = 500000.0
ROPE_FACTOR = 8.0
LOW_FREQ = 1.0
HIGH_FREQ = 4.0
INITIAL_SPAN = 8192.0
NORM_EPSILON = 1e-05
MASKED = -1e30


def inverse_freqs(head_width):
    pair_index = jnp.arange(head_width // 2, dtype=jnp.float32)
    base_freq = ROPE_BASE ** (-2.0 * pair_index / head_width)
    wavelength = 2.0 * math.pi / base_freq
    smooth = (INITIAL_SPAN / wavelength - LOW_FREQ) / (HIGH_FREQ - LOW_FREQ)
    blended = (1.0 - smooth) * base_freq / ROPE_FACTOR + smooth * base_freq
    return jnp.where(
        wavelength < INITIAL_SPAN / HIGH_FREQ,
        base_freq,
        jnp.where(wavelength > INITIAL_SPAN / LOW_FREQ, base_freq / ROPE_FACTOR, blended),
    )


def rotate(vectors, positions):
    head_width = vectors.shape[-1]
    angles = positions[..., None] * inverse_freqs(head_width)
    cosine = jnp.cos(angles)
    sinus = jnp.sin(angles)
    first_half = vectors[..., : head_width // 2]
    second_half = vectors[..., head_width // 2 :]
    return jnp.concatenate(
        [first_half * cosine - second_half * sinus, second_half * cosine + first_half * sinus],
        axis=-1,
    )


def visibility(key_labels, is_prefix, key_pos, query_segs, query_index):
    earlier = key_labels[None, :] <= query_segs[:, None]
    same = (key_labels[None, :] == query_segs[:, None]) & (key_pos[None, :] <= query_index[:, None])
    return jnp.where(is_prefix[None, :], earlier, same)


def update(carry, grouped, key_block, value_block, seen):
    running_max, totals, numerator = carry
    scores = jnp.einsum("hrd,hnd->hrn", grouped, key_block, preferred_element_type=jnp.float32) * (
        1.0 / math.sqrt(HD)
    )
    scores = jnp.where(seen[None], scores, MASKED)
    new_max = jnp.maximum(running_max, jnp.max(scores, axis=2))
    weights = jnp.where(seen[None], jnp.exp(scores - new_max[..., None]), 0.0)
    totals = jnp.sum(weights, axis=2)
    numerator = jnp.einsum(
        "hrn,hnd->hrd",
        weights.astype(jnp.bfloat16),
        value_block,
        preferred_element_type=jnp.float32,
    )
    return (new_max, totals, numerator)


def empty_state(kv_heads, row_count):
    return (
        jnp.full((kv_heads, row_count), MASKED, jnp.float32),
        jnp.zeros((kv_heads, row_count), jnp.float32),
        jnp.zeros((kv_heads, row_count, HD), jnp.float32),
    )


def per_device(
    stream,
    pending,
    norm_gain,
    w_query,
    w_key,
    w_value,
    w_out,
    prefix_keys,
    prefix_values,
    prefix_segments,
    stretch_segments,
    stretch_offset,
):
    tok_rows = stream.shape[0]
    prefix_rows = prefix_keys.shape[1]
    ctx_index = lax.axis_index("ctx")
    tp_index = lax.axis_index("tp")
    gain_wide = norm_gain.astype(jnp.float32)
    whole = lax.all_gather(stream, "tp", axis=1, tiled=True).astype(jnp.float32)
    mean_square = jnp.mean(whole * whole, axis=1, keepdims=True)
    normed = (whole * lax.rsqrt(mean_square + NORM_EPSILON) * gain_wide).astype(jnp.bfloat16)
    q_cols = w_query.shape[1]
    q_heads = q_cols // HD
    full_group = HQ // KVH
    kv_heads = max(1, q_heads // full_group)
    group_size = q_heads // kv_heads
    head_start = tp_index * q_heads // full_group
    kv_cols = kv_heads * HD
    key_slice = lax.dynamic_slice_in_dim(w_key, head_start * HD, kv_cols, 1)
    value_slice = lax.dynamic_slice_in_dim(w_value, head_start * HD, kv_cols, 1)
    pieces = (
        lax.all_gather(w_query, "ctx", axis=0, tiled=True),
        lax.all_gather(key_slice, "ctx", axis=0, tiled=True),
        lax.all_gather(value_slice, "ctx", axis=0, tiled=True),
    )
    query_raw, key_full, value_full = tuple(
        (jnp.dot(normed, piece_rows, preferred_element_type=jnp.float32) for piece_rows in pieces)
    )
    token_index = ctx_index * tok_rows + jnp.arange(tok_rows, dtype=jnp.int32)
    positions = stretch_offset[0].astype(jnp.float32) + token_index.astype(jnp.float32)
    query_rows = rotate(query_raw.reshape(tok_rows, q_heads, HD), positions[:, None]).astype(
        jnp.bfloat16
    )
    new_keys = jnp.transpose(
        rotate(key_full.reshape(tok_rows, kv_heads, HD), positions[:, None]).astype(jnp.bfloat16),
        (1, 0, 2),
    )
    new_values = jnp.transpose(
        value_full.astype(jnp.bfloat16).reshape(tok_rows, kv_heads, HD), (1, 0, 2)
    )
    old_keys = lax.dynamic_slice_in_dim(prefix_keys, head_start, kv_heads, 0)
    old_values = lax.dynamic_slice_in_dim(prefix_values, head_start, kv_heads, 0)
    local_keys = jnp.concatenate([old_keys, new_keys], 1)
    local_values = jnp.concatenate([old_values, new_values], 1)
    key_labels = jnp.concatenate([prefix_segments, stretch_segments])
    key_span = prefix_rows + tok_rows
    grouped = jnp.transpose(
        query_rows.reshape(tok_rows, kv_heads, group_size, HD), (1, 0, 2, 3)
    ).reshape(kv_heads, tok_rows * group_size, HD)
    query_index = jnp.repeat(token_index, group_size)
    query_segs = jnp.repeat(stretch_segments, group_size)
    both = jnp.stack([local_keys, local_values])
    kv_block = lax.all_gather(both, "ctx", axis=2, tiled=True)
    label_block = lax.all_gather(key_labels[None, None, :], "ctx", axis=2, tiled=True)
    key_count = kv_block.shape[2]
    absolute = jnp.arange(key_count, dtype=jnp.int32)
    within = absolute % key_span
    key_pos = absolute // key_span * tok_rows + within - prefix_rows
    seen = visibility(label_block[0, 0], within < prefix_rows, key_pos, query_segs, query_index)
    running_max, totals, numerator = update(
        empty_state(kv_heads, tok_rows * group_size), grouped, kv_block[0], kv_block[1], seen
    )
    attended_heads = (numerator / totals[..., None]).astype(jnp.bfloat16)
    attended = jnp.transpose(
        attended_heads.reshape(kv_heads, tok_rows, group_size, HD), (1, 0, 2, 3)
    ).reshape(tok_rows, q_cols)
    head_terms = jnp.dot(
        attended,
        lax.all_gather(w_out, "ctx", axis=1, tiled=True),
        preferred_element_type=jnp.float32,
    )
    head_share, pending_share = (
        lax.psum_scatter(
            head_terms.astype(jnp.bfloat16), "tp", scatter_dimension=1, tiled=True
        ).astype(jnp.float32),
        lax.psum_scatter(
            pending[0].astype(jnp.float32).astype(jnp.bfloat16),
            "tp",
            scatter_dimension=1,
            tiled=True,
        ).astype(jnp.float32),
    )
    block_share = head_share + pending_share
    return (stream.astype(jnp.float32) + block_share).astype(jnp.bfloat16)


def solution(mesh):
    in_specs = (
        P("ctx", "tp"),
        P("tp", "ctx", None),
        P(),
        P("ctx", "tp"),
        P("ctx", None),
        P("ctx", None),
        P("tp", "ctx"),
        P(None, "ctx", None),
        P(None, "ctx", None),
        P("ctx"),
        P("ctx"),
        P(),
    )
    out_specs = P("ctx", "tp")
    return jax.shard_map(
        per_device, mesh=mesh, in_specs=in_specs, out_specs=out_specs, check_vma=False
    )
```

profile of v0, /device:TPU:4, one launch (start us, length us, event | category | flops | bytes accessed | tf_op | source)
XLA Modules:
  0.0 763.9 jit_solution(7365348122531664401)
XLA Ops:
  6.5 0.0 copy-start
  6.5 0.0 all-gather.9.cloned.1.call-start
  6.5 0.7 all-gather.9.cloned.1.call-update
  7.3 0.0 all-gather.13.cloned.1.call-start
  7.3 0.4 copy-done
  7.8 0.7 constant_dynamic-slice_fusion.2
  8.5 0.0 all-gather.13.cloned.1.call-update
  8.5 0.0 all-gather.15.cloned.1.call-start
  8.5 1.6 constant_dynamic-slice_fusion
  10.1 0.0 all-gather.15.cloned.1.call-update
  10.1 0.0 all-gather.11.cloned.1.call-start
  10.2 0.5 all-gather.11.cloned.1.call-update
  10.7 0.0 all-gather.17.cloned.1.call-start
  10.8 0.7 convert_element_type.65
  12.2 1.1 constant_dynamic-slice_fusion.1
  13.3 139.6 %all-gather.9.cloned.1.call-done = bf16[384,8192]{1,0:T(8,128)(2,1)} async-done(((bf16[384,512]{1,0:T(8,128)(2,1)}), bf16[384,8192]{1,0:T(8,128)(2,1)}) %all-gather.9.cloned.1.call-update) | async-done | bytes 6291472 | tf_op jit(solution)/shard_map/all_gather | solution.py:99
  152.8 4.1 fusion.5
  156.9 49.4 %all-gather.13.cloned.1.call-done = bf16[8192,128]{1,0:T(8,128)(2,1)} async-done(((bf16[512,128]{1,0:T(8,128)(2,1)}), bf16[8192,128]{1,0:T(8,128)(2,1)}) %all-gather.13.cloned.1.call-update) | async-done | bytes 2097168 | tf_op jit(solution)/shard_map/all_gather | solution.py:113
  206.3 5.5 convolution_bitcast_fusion
  211.9 0.5 fusion.37
  212.3 0.0 copy-start.3
  212.4 0.1 copy.19
  212.5 0.0 copy-start.4
  212.5 48.0 %all-gather.15.cloned.1.call-done = bf16[8192,128]{1,0:T(8,128)(2,1)} async-done(((bf16[512,128]{1,0:T(8,128)(2,1)}), bf16[8192,128]{1,0:T(8,128)(2,1)}) %all-gather.15.cloned.1.call-update) | async-done | bytes 2097168 | tf_op jit(solution)/shard_map/all_gather | solution.py:114
  260.6 5.2 fusion.9
  265.9 0.9 pad_maximum_fusion
  266.7 0.0 all-gather.17.cloned.1.call-update
  266.8 0.0 all-gather.19.cloned.1.call-start
  266.8 0.5 all-gather.19.cloned.1.call-update
  267.3 0.0 reduce-scatter.5.cloned.1.call-start
  267.4 0.7 reduce-scatter.5.cloned.1.call-update
  268.1 0.0 reduce-scatter.3.cloned.1.call-start
  268.1 0.8 multiply_cosine_fusion
  269.0 0.1 broadcast_in_dim.40
  269.1 0.1 le.38
  269.3 0.0 copy-done.3
  269.3 0.1 broadcast_in_dim.39
  269.4 0.1 le.34
  269.6 0.0 copy-done.4
  269.6 22.4 %all-gather.1 = s32[16,1,1152]{2,1,0:T(1,128)S(1)} all-gather(s32[1,1,1152]{2,1,0:T(1,128)S(1)} %reshape.264), channel_id=2, replica_groups=mesh['ctx'=16,'tp'=16] {'ctx'}, dimensions={0}, use_global_device_ids=true | all-gather | bytes 78336 | tf_op jit(solution)/shard_map/all_gather | solution.py:144
  292.0 30.4 %all-gather.11.cloned.1.call-done = bf16[8192,256]{1,0:T(8,128)(2,1)} async-done(((bf16[512,256]{1,0:T(8,128)(2,1)}), bf16[8192,256]{1,0:T(8,128)(2,1)}) %all-gather.11.cloned.1.call-update) | async-done | bytes 4194320 | tf_op jit(solution)/shard_map/all_gather | solution.py:112
  322.5 6.6 fusion.44
  329.1 0.2 copy.20
  329.3 0.2 copy.21
  329.5 0.4 subtract_convert_fusion
  329.9 75.6 %all-gather.17.cloned.1.call-done = bf16[2,1,18432,128]{3,2,1,0:T(8,128)(2,1)} async-done(((bf16[2,1,1152,128]{3,2,1,0:T(8,128)(2,1)}), bf16[2,1,18432,128]{3,2,1,0:T(8,128)(2,1)}) %all-gather.17.cloned.1.call-update) | async-done | bytes 9437200 | tf_op jit(solution)/shard_map/all_gather | solution.py:143
  405.5 30.0 %fusion = (f32[768]{0:T(1024)S(1)}, f32[768,18432]{1,0:T(8,128)}) fusion(s32[768]{0:T(1024)S(1)} %le.38, s32[18432]{0:T(1024)S(1)} %fusion.29, s32[768]{0:T(1024)S(1)} %le.34, s32[18432]{0:T(1024)S(1)} %bitcast.37, pred[18432]{0:T(1024)(128)(4,1)S(1)} %fusion.33, bf16[2,1,18432,128]{3,2,1,0:T(8,128)(2,1)} %all-gather.17.cloned.1.call-done, ...), kind=kOutput, calls=%fused_computation.3 | convolution fusion | flops 3737517312 | bytes 61713408 | tf_op jit(solution)/shard_map/hrd,hnd->hrn/dot_general | solution.py:56
  435.4 39.6 %fusion.1 = f32[768]{0:T(1024)S(1)} fusion(f32[768,18432]{1,0:T(8,128)} %get-tuple-element.14, f32[768]{0:T(1024)S(1)} %broadcast_maximum_fusion, s32[768]{0:T(1024)S(1)} %le.38, s32[18432]{0:T(1024)S(1)} %fusion.29, s32[768]{0:T(1024)S(1)} %le.34, s32[18432]{0:T(1024)S(1)} %bitcast.38, pred[18432]{0:T(1024)(128)(4,1)S(1)} %fusion.33), kind=kLoop, calls=%fused_computation.4 | loop fusion | flops 141556992 | bytes 56801280 | tf_op jit(solution)/shard_map/reduce_sum | solution.py:62
  475.0 0.0 copy-start.1
  475.0 34.2 %fusion.13 = bf16[768,128]{1,0:T(8,128)(2,1)S(1)} fusion(bf16[2,1,18432,128]{3,2,1,0:T(8,128)(2,1)} %all-gather.17.cloned.1.call-done, f32[768,18432]{1,0:T(8,128)} %get-tuple-element.14, f32[768]{0:T(1024)S(1)} %broadcast_maximum_fusion, f32[768]{0:T(1024)S(1)} %fusion.1, s32[18432]{0:T(1024)S(1)} %bitcast.39, s32[18432]{0:T(1024)S(1)} %fusion.29, ...), kind=kOutput, calls=%fused_computation.20 | convolution fusion | flops 3765633024 | bytes 61716480 | tf_op jit(solution)/shard_map/hrn,hnd->hrd/dot_general | solution.py:63
  509.3 0.0 copy-start.2
  509.3 0.1 reshape_transpose_reshape.4
  509.3 0.0 all-gather.19.cloned.1.call-done
  509.4 6.7 convolution_convert_fusion
  516.1 0.0 reduce-scatter.3.cloned.1.call-update
  516.1 94.9 %reduce-scatter.5.cloned.1.call-done = bf16[384,512]{1,0:T(8,128)(2,1)} async-done(((bf16[384,8192]{1,0:T(8,128)(2,1)}), bf16[384,512]{1,0:T(8,128)(2,1)}) %reduce-scatter.5.cloned.1.call-update) | async-done | bytes 393232 | tf_op jit(solution)/shard_map/reduce_scatter | solution.py:166
  611.1 144.0 %reduce-scatter.3.cloned.1.call-done = bf16[384,512]{1,0:T(8,128)(2,1)} async-done(((bf16[384,8192]{1,0:T(8,128)(2,1)}), bf16[384,512]{1,0:T(8,128)(2,1)}) %reduce-scatter.3.cloned.1.call-update) | async-done | bytes 393232 | tf_op jit(solution)/shard_map/reduce_scatter | solution.py:163
  755.0 0.0 copy-done.2
  755.0 2.0 add_convert_fusion
  757.0 0.0 copy-done.1
  (13 shorter events, 0.2 us)
Async XLA Ops:
  6.5 1.2 copy-start
  6.5 146.3 %all-gather.9.cloned.1.call-start = ((), (), s32[]{:S(2)}) async-start(), calls=%async_computation.2 | async-start | bytes 6684672 | tf_op jit(solution)/shard_map/all_gather | solution.py:99
  7.3 199.1 %all-gather.13.cloned.1.call-start = ((), (), s32[]{:S(2)}) async-start(), calls=%async_computation.4 | async-start | bytes 2228224 | tf_op jit(solution)/shard_map/all_gather | solution.py:113
  8.5 252.1 %all-gather.15.cloned.1.call-start = ((), (), s32[]{:S(2)}) async-start(), calls=%async_computation.5 | async-start | bytes 2228224 | tf_op jit(solution)/shard_map/all_gather | solution.py:114
  10.1 312.3 %all-gather.11.cloned.1.call-start = ((), (), s32[]{:S(2)}) async-start(), calls=%async_computation.3 | async-start | bytes 4456448 | tf_op jit(solution)/shard_map/all_gather | solution.py:112
  10.7 394.8 %all-gather.17.cloned.1.call-start = ((), (), s32[]{:S(2)}) async-start(), calls=%async_computation.6 | async-start | bytes 10027008 | tf_op jit(solution)/shard_map/all_gather | solution.py:143
  212.3 56.9 %copy-start.3 = (s32[384]{0:T(512)S(1)}, s32[384]{0:T(512)}, u32[]{:S(2)}) copy-start(s32[384]{0:T(512)} %param.22) | copy-start | bytes 4612
  212.5 57.0 %copy-start.4 = (s32[768]{0:T(1024)S(1)}, s32[768]{0:T(1024)}, u32[]{:S(2)}) copy-start(s32[768]{0:T(1024)} %param.21) | copy-start | bytes 9220
  266.8 242.6 %all-gather.19.cloned.1.call-start = ((), (), s32[]{:S(2)}) async-start(), calls=%async_computation.7 | async-start | bytes 4456448 | tf_op jit(solution)/shard_map/all_gather | solution.py:159
  267.3 343.7 %reduce-scatter.5.cloned.1.call-start = ((), (), s32[]{:S(2)}) async-start(), calls=%async_computation.9 | async-start | bytes 6684672 | tf_op jit(solution)/shard_map/reduce_scatter | solution.py:166
  268.1 486.9 %reduce-scatter.3.cloned.1.call-start = ((), (), s32[]{:S(2)}) async-start(), calls=%async_computation.8 | async-start | bytes 6684672 | tf_op jit(solution)/shard_map/reduce_scatter | solution.py:163
  475.0 282.0 %copy-start.1 = (bf16[512,1024]{1,0:T(8,128)(2,1)S(1)}, bf16[512,1024]{1,0:T(8,128)(2,1)}, u32[]{:S(2)}) copy-start(bf16[512,1024]{1,0:T(8,128)(2,1)} %param.16) | copy-start | bytes 3145732
  509.3 245.8 %copy-start.2 = (bf16[384,512]{1,0:T(8,128)(2,1)S(1)}, bf16[384,512]{1,0:T(8,128)(2,1)}, u32[]{:S(2)}) copy-start(bf16[384,512]{1,0:T(8,128)(2,1)} %param.12) | copy-start | bytes 1179652
Sparse Core Ops, SparseCore 0:
  9.2 143.6 all-gather.8
  155.6 50.6 all-gather.12
  209.1 51.4 all-gather.14
  263.2 59.2 all-gather.10
  325.1 80.3 all-gather.16
  408.0 59.5 all-gather.18
  470.1 140.8 reduce-scatter.4
  613.6 141.3 reduce-scatter.2
where the time goes:
time: 764 us
  waiting for transfers between devices  584 us (76%)
  matrix products  88.3 us (12%)
  other arithmetic  49.1 us (6%)
  blocking collectives  22.4 us (3%)
  between operations  14.4 us (2%)
    reduce_scatter x1, waiting for transfers between devices, per_device(): lax.psum_scatter(head_terms.astype(jnp.bfloat16), 'tp', scatter_dimension...  144 us
    all_gather x1, waiting for transfers between devices, per_device(): whole = lax.all_gather(stream, 'tp', axis=1, tiled=True).astype(jnp.float32)  140 us
    reduce_scatter x1, waiting for transfers between devices, per_device(): lax.psum_scatter(pending[0].astype(jnp.float32).astype(jnp.bfloat16), 'tp...  94.9 us
    all_gather x1, waiting for transfers between devices, per_device(): kv_block = lax.all_gather(both, 'ctx', axis=2, tiled=True)  75.6 us
    all_gather x1, waiting for transfers between devices, per_device(): lax.all_gather(key_slice, 'ctx', axis=0, tiled=True)  49.4 us
    all_gather x1, waiting for transfers between devices, per_device(): lax.all_gather(value_slice, 'ctx', axis=0, tiled=True)  48 us
    reduce_sum x1, other arithmetic, update(): totals = jnp.sum(weights, axis=2)  39.6 us
    dot_general x1, matrix products, update(): jnp.einsum('hrn,hnd->hrd', weights.astype(jnp.bfloat16), value_block, pre...  34.2 us
  transfers between devices with their start and end apart: 8, of which 7 were waited for; matrix products, arithmetic and copies ran while one was open for 18% of the time, Pallas kernels for 0%

commit v1 on v0

v1 whole, which is shorter than its diff:
```python
import functools
import math

import jax
import jax.numpy as jnp
from jax import lax
from jax.experimental import pallas as pl
from jax.experimental.pallas import tpu as pltpu
from jax.sharding import PartitionSpec as P

MESH = pl.DeviceIdType.MESH
HD = 128
ROPE_BASE = 500000.0
ROPE_FACTOR = 8.0
LOW_FREQ = 1.0
HIGH_FREQ = 4.0
INITIAL_SPAN = 8192.0
NORM_EPSILON = 1e-05
MASKED = -1e30
LABEL_ROWS = 16


def inverse_freqs(head_width):
    pair_index = jnp.arange(head_width // 2, dtype=jnp.float32)
    base_freq = ROPE_BASE ** (-2.0 * pair_index / head_width)
    wavelength = 2.0 * math.pi / base_freq
    smooth = (INITIAL_SPAN / wavelength - LOW_FREQ) / (HIGH_FREQ - LOW_FREQ)
    blended = (1.0 - smooth) * base_freq / ROPE_FACTOR + smooth * base_freq
    return jnp.where(
        wavelength < INITIAL_SPAN / HIGH_FREQ,
        base_freq,
        jnp.where(wavelength > INITIAL_SPAN / LOW_FREQ, base_freq / ROPE_FACTOR, blended),
    )


def coords():
    c = lax.axis_index("ctx")
    t = lax.axis_index("tp")
    return c // 4, (c // 2) % 2, c % 2, t // 2, t % 2


def ctx_of(y, xh, core):
    return (y * 2 + xh) * 2 + core


def tp_of(z, xl):
    return z * 2 + xl


def neighbours():
    y, xh, core, z, xl = coords()
    here = ctx_of(y, xh, core)
    mine = tp_of(z, xl)
    return {
        "z+": (here, tp_of((z + 1) % 8, xl)),
        "z-": (here, tp_of((z + 7) % 8, xl)),
        "xl": (here, tp_of(z, 1 - xl)),
        "y+": (ctx_of((y + 1) % 4, xh, core), mine),
        "y-": (ctx_of((y + 3) % 4, xh, core), mine),
        "xh": (ctx_of(y, 1 - xh, core), mine),
        "xd": (ctx_of(y, 1 - xh, core), tp_of(z, 1 - xl)),
        "sib": (ctx_of(y, xh, 1 - core), mine),
    }


def greet(devices):
    barrier = pltpu.get_barrier_semaphore()
    for device in devices:
        pl.semaphore_signal(barrier, inc=1, device_id=device, device_id_type=MESH)
    pl.semaphore_wait(barrier, len(devices))


class Net:
    def __init__(self, links, send_sem, recv_sem):
        self.links, self.send_sem, self.recv_sem = links, send_sem, recv_sem
        self.copies = []

    def push(self, src, link, dst=None):
        k = len(self.copies)
        copy = pltpu.make_async_remote_copy(
            src_ref=src,
            dst_ref=src if dst is None else dst,
            send_sem=self.send_sem.at[k],
            recv_sem=self.recv_sem.at[k],
            device_id=self.links[link] if isinstance(link, str) else link,
            device_id_type=MESH,
        )
        copy.start()
        self.copies.append(copy)
        return copy

    def drain(self):
        for copy in self.copies:
            copy.wait_send()


class TpRing:
    def __init__(self, net, own, buf):
        self.net, self.buf = net, buf
        rows = own.shape[0]
        half, quarter = rows // 2, rows // 4
        self.low, self.high = pl.ds(0, half), pl.ds(half, half)
        self.parts = (pl.ds(half, quarter), pl.ds(half + quarter, quarter))
        _, _, _, z, xl = coords()
        t = tp_of(z, xl)
        self.swap = net.push(own.at[self.low], "xl", buf.at[t, self.low])
        self.hop = {}
        for way in ("z+", "z-"):
            self.hop[way, "own"] = net.push(own.at[self.low], way, buf.at[t, self.low])
            self.hop[way, "high"] = net.push(own.at[self.high], way, buf.at[t, self.high])
        self.across = [net.push(own.at[self.high], "xl", buf.at[t, self.high])]

    def cross(self):
        _, _, _, z, xl = coords()
        self.swap.wait_recv()
        for way in ("z+", "z-"):
            self.hop[way, "other"] = self.net.push(self.buf.at[tp_of(z, 1 - xl), self.low], way)

    def step(self, step):
        _, _, _, z, xl = coords()
        push, buf, hop = self.net.push, self.buf, self.hop
        for way, sign in (("z+", -1), ("z-", 1)):
            at = (z + sign * step + 8) % 8
            mine, theirs = tp_of(at, xl), tp_of(at, 1 - xl)
            part = 0 if way == "z+" else 1
            if step < 4:
                hop[way, "own"].wait_recv()
                if step < 3 or part == 0:
                    hop[way, "own"] = push(buf.at[mine, self.low], way)
                hop[way, "high"].wait_recv()
                rows = self.high if step < 3 else self.parts[part]
                hop[way, "high"] = push(buf.at[mine, rows], way)
                self.across.append(push(buf.at[mine, self.high], "xl"))
                hop[way, "other"].wait_recv()
                if step < 3 or part == 1:
                    hop[way, "other"] = push(buf.at[theirs, self.low], way)
            else:
                hop[way, "own" if part == 0 else "other"].wait_recv()
                hop[way, "high"].wait_recv()
                self.across.append(push(buf.at[mine, self.parts[part]], "xl"))

    def finish(self):
        for copy in self.across:
            copy.wait_recv()


class CtxRing:
    def __init__(self, net, own, buf, side_link):
        self.net, self.own, self.buf = net, own, buf
        y, xh, core, _, _ = coords()
        self.c, self.beside = ctx_of(y, xh, core), ctx_of(y, 1 - xh, core)
        self.side = net.push(own, side_link, buf.at[self.c])
        self.sib = [net.push(own, "sib", buf.at[self.c])]
        self.hop = {}

    def send_own(self):
        for way in ("y+", "y-"):
            self.hop[way, "own"] = self.net.push(self.own, way, self.buf.at[self.c])

    def send_side(self):
        self.side.wait_recv()
        for way in ("y+", "y-"):
            self.hop[way, "side"] = self.net.push(self.buf.at[self.beside], way)
        self.sib.append(self.net.push(self.buf.at[self.beside], "sib"))

    def step(self, step):
        y, xh, core, _, _ = coords()
        push, buf, hop = self.net.push, self.buf, self.hop
        for way, sign in (("y+", -1), ("y-", 1)):
            at = (y + sign * step + 4) % 4
            own, beside = ctx_of(at, xh, core), ctx_of(at, 1 - xh, core)
            first = way == "y+"
            if step == 1:
                hop[way, "own"].wait_recv()
                if first:
                    hop[way, "own"] = push(buf.at[own], way)
                self.sib.append(push(buf.at[own], "sib"))
                hop[way, "side"].wait_recv()
                if not first:
                    hop[way, "side"] = push(buf.at[beside], way)
                self.sib.append(push(buf.at[beside], "sib"))
            else:
                hop[way, "own" if first else "side"].wait_recv()
                self.sib.append(push(buf.at[own if first else beside], "sib"))

    def finish(self):
        for copy in self.sib:
            copy.wait_recv()


FRONT_COPIES = 96


def front_kernel(
    stream, weight, old, w_out, gain, cosine, sinus,
    query, cache, fresh, out_rows,
    blocks, weights, totals, squares, made, turned,
    local_sem, send_sem, recv_sem, turn_sem,
):
    y, xh, core, z, xl = coords()
    c, t = ctx_of(y, xh, core), tp_of(z, xl)
    links = neighbours()
    later = {}
    for ahead in (1, 2):
        for other in (0, 1):
            later[ahead, other] = ((c + ahead) % 16, tp_of(z, (xl + other) % 2))
    earlier = [
        ((c + 16 - ahead) % 16, tp_of(z, (xl + other) % 2)) for ahead in (1, 2) for other in (0, 1)
    ]
    barrier = pltpu.get_barrier_semaphore()

    @pl.when(c != t)
    def _():
        pl.semaphore_signal(barrier, inc=1, device_id=(t, c), device_id_type=MESH)

    local = [
        pltpu.make_async_copy(stream, blocks.at[t], local_sem.at[0]),
        pltpu.make_async_copy(weight, weights.at[c], local_sem.at[1]),
        pltpu.make_async_copy(old, cache.at[c], local_sem.at[2]),
    ]
    peers = list(links.values()) + list(later.values()) + earlier
    for device in peers:
        pl.semaphore_signal(barrier, inc=1, device_id=device, device_id_type=MESH)

    @pl.when(c != t)
    def _():
        pl.semaphore_wait(barrier, len(peers) + 1)

    @pl.when(c == t)
    def _():
        pl.semaphore_wait(barrier, len(peers))

    net = Net(links, send_sem, recv_sem)
    tp_ring = TpRing(net, stream, blocks)
    w_ring = CtxRing(net, weight, weights, "xh")
    w_ring.send_own()
    old_ring = CtxRing(net, old, cache, "xd")
    for copy in local:
        copy.start()
    turn = pltpu.make_async_remote_copy(
        src_ref=w_out,
        dst_ref=turned,
        send_sem=turn_sem.at[0],
        recv_sem=turn_sem.at[1],
        device_id=(t, c),
        device_id_type=MESH,
    )
    stay = pltpu.make_async_copy(w_out, turned, turn_sem.at[2])

    @pl.when(c != t)
    def _():
        turn.start()

    @pl.when(c == t)
    def _():
        stay.start()

    tp_ring.cross()
    w_ring.send_side()
    tp_ring.step(1)
    w_ring.step(1)
    old_ring.send_own()
    old_ring.send_side()
    tp_ring.step(2)
    w_ring.step(2)
    tp_ring.step(3)
    old_ring.step(1)

    @pl.when(c != t)
    def _():
        turn.wait_send()
        turn.wait_recv()

    @pl.when(c == t)
    def _():
        stay.wait()

    out_ring = CtxRing(net, turned, out_rows, "xh")
    out_ring.send_own()
    out_ring.send_side()
    own_out = pltpu.make_async_copy(turned, out_rows.at[c], local_sem.at[3])
    own_out.start()
    tp_ring.step(4)
    old_ring.step(2)
    w_ring.finish()
    tp_ring.finish()
    local[0].wait()
    local[1].wait()

    totals[...] = jnp.zeros_like(totals)
    squares[...] = jnp.zeros_like(squares)

    def project(b, _):
        wide = blocks[b].astype(jnp.float32)
        part = wide * wide
        squares[...] += sum(part[:, k * HD : (k + 1) * HD] for k in range(part.shape[1] // HD))
        low = (wide * gain[b]).astype(jnp.bfloat16)
        totals[...] += jnp.dot(low, weights[b], preferred_element_type=jnp.float32)
        return 0

    lax.fori_loop(0, 16, project, 0)
    width = 16 * stream.shape[1]
    mean_square = jnp.sum(squares[...], axis=1, keepdims=True) / width
    scale = lax.rsqrt(mean_square + NORM_EPSILON)
    cos, sin = cosine[...], sinus[...]

    def rotate(part):
        return part * cos + pltpu.roll(part, HD // 2, 1) * sin

    to_exponent = math.log2(math.e) / math.sqrt(HD)
    for h in range(2):
        part = totals[:, h * HD : (h + 1) * HD] * scale
        query[h] = (rotate(part) * to_exponent).astype(jnp.bfloat16)
    part = totals[:, 2 * HD :] * scale

    @pl.when(xl == 0)
    def _():
        made[...] = rotate(part).astype(jnp.bfloat16)

    @pl.when(xl == 1)
    def _():
        made[...] = part.astype(jnp.bfloat16)

    keep = pltpu.make_async_copy(made, fresh.at[xl, 2], local_sem.at[4])
    keep.start()
    sent = [net.push(made, "xl", fresh.at[xl, 2])]
    for (ahead, _), device in later.items():
        sent.append(net.push(made, device, fresh.at[xl, 2 - ahead]))

    old_ring.finish()
    out_ring.step(1)
    out_ring.step(2)
    out_ring.finish()
    for copy in sent:
        copy.wait_recv()
    keep.wait()
    local[2].wait()
    own_out.wait()
    net.drain()
    assert len(net.copies) <= FRONT_COPIES


def front(stream, weight, old, w_out, gain, cosine, sinus):
    rows, cols = stream.shape
    low = jnp.bfloat16
    any_spec = pl.BlockSpec(memory_space=pl.ANY)
    vmem = pl.BlockSpec(memory_space=pltpu.VMEM)
    return pl.pallas_call(
        front_kernel,
        out_shape=(
            jax.ShapeDtypeStruct((2, rows, HD), low),
            jax.ShapeDtypeStruct((16, *old.shape), low),
            jax.ShapeDtypeStruct((2, 3, rows, HD), low),
            jax.ShapeDtypeStruct((16, *w_out.shape), low),
        ),
        in_specs=[any_spec] * 4 + [vmem] * 3,
        out_specs=[vmem] + [any_spec] * 3,
        scratch_shapes=[
            pltpu.VMEM((16, rows, cols), low),
            pltpu.VMEM((16, *weight.shape), low),
            pltpu.VMEM((rows, weight.shape[1]), jnp.float32),
            pltpu.VMEM((rows, HD), jnp.float32),
            pltpu.VMEM((rows, HD), low),
            pltpu.VMEM(w_out.shape, low),
            pltpu.SemaphoreType.DMA((5,)),
            pltpu.SemaphoreType.DMA((FRONT_COPIES,)),
            pltpu.SemaphoreType.DMA((FRONT_COPIES,)),
            pltpu.SemaphoreType.DMA((3,)),
        ],
        compiler_params=pltpu.CompilerParams(
            collective_id=0, has_side_effects=True, vmem_limit_bytes=40 << 20
        ),
        name="front",
    )(stream, weight, old, w_out, gain, cosine, sinus)


def attend_kernel(query, fresh, marks, q_marks, old, result, top, total, mix):
    step = pl.program_id(0)
    c = lax.axis_index("ctx")
    heads, rows, _ = query.shape
    span = (old.shape[1] - LABEL_ROWS) // 2

    @pl.when(step == 0)
    def _():
        top[...] = jnp.full_like(top, MASKED)
        total[...] = jnp.zeros_like(total)
        mix[...] = jnp.zeros_like(mix)

    def absorb(h, keys, values, seen):
        scores = lax.dot_general(
            query[h], keys, (((1,), (1,)), ((), ())), preferred_element_type=jnp.float32
        )
        scores = jnp.where(seen, scores, MASKED)
        before = top[h]
        now = jnp.maximum(before, jnp.max(scores, axis=1, keepdims=True))
        fade = jnp.exp2(before - now)
        weights = jnp.exp2(scores - now[:, :1])
        total[h] = total[h] * fade + jnp.sum(weights, axis=1, keepdims=True)
        mix[h] = mix[h] * fade + jnp.dot(
            weights.astype(jnp.bfloat16), values, preferred_element_type=jnp.float32
        )
        top[h] = now

    def row_of(labels, count):
        wide = labels.astype(jnp.float32)
        return jnp.concatenate([wide[k : k + 1] for k in range(count)], axis=1)

    own = q_marks[...]
    prefix_marks = row_of(old[0, 2 * span :], span // HD)
    seen = prefix_marks <= own
    for h in range(heads):
        absorb(h, old[0, :span], old[0, span : 2 * span], seen)

    @pl.when(step == pl.num_programs(0) - 1)
    def _():
        first = span // HD
        for j in range(3):
            back = 2 - j
            labels = marks[(c + 16 - back) % 16].astype(jnp.float32)
            row = jnp.concatenate(
                [labels[first + k : first + k + 1] for k in range(rows // HD)], axis=1
            )
            row = jnp.where(c >= back, row, -1.0)
            same = row == own
            if back == 0:
                at = lax.broadcasted_iota(jnp.int32, (rows, rows), 0)
                key_at = lax.broadcasted_iota(jnp.int32, (rows, rows), 1)
                same = same & (key_at <= at)
            for h in range(heads):
                absorb(h, fresh[0, j], fresh[1, j], same)
        for h in range(heads):
            result[:, h * HD : (h + 1) * HD] = (mix[h] / total[h]).astype(jnp.bfloat16)


def attend(query, fresh, q_marks, cache):
    heads, rows, _ = query.shape
    span = cache.shape[1]
    return pl.pallas_call(
        attend_kernel,
        grid=(16,),
        out_shape=jax.ShapeDtypeStruct((rows, heads * HD), jnp.bfloat16),
        in_specs=[
            pl.BlockSpec(query.shape, lambda i: (0, 0, 0)),
            pl.BlockSpec(fresh.shape, lambda i: (0, 0, 0, 0)),
            pl.BlockSpec((16, LABEL_ROWS, HD), lambda i: (0, span // LABEL_ROWS - 1, 0)),
            pl.BlockSpec((rows, 1), lambda i: (0, 0)),
            pl.BlockSpec((1, span, HD), lambda i: (i, 0, 0)),
        ],
        out_specs=pl.BlockSpec((rows, heads * HD), lambda i: (0, 0)),
        scratch_shapes=[pltpu.VMEM((heads, rows, HD), jnp.float32) for _ in range(3)],
        compiler_params=pltpu.CompilerParams(vmem_limit_bytes=40 << 20),
        cost_estimate=pl.CostEstimate(
            flops=4 * heads * rows * 13440 * HD, bytes_accessed=7 << 20, transcendentals=heads * rows * 13440
        ),
        name="attend",
    )(query, fresh, cache, q_marks, cache)


BACK_COPIES = 40


def back_kernel(attended, out_rows, block, gathered, rows_here, local_sem, send_sem, recv_sem):
    _, _, _, z, xl = coords()
    t = tp_of(z, xl)
    links = neighbours()
    load = pltpu.make_async_copy(out_rows, rows_here, local_sem.at[0])
    load.start()
    gathered[t] = attended[...]
    greet([links[name] for name in ("z+", "z-", "xl")])
    net = Net(links, send_sem, recv_sem)
    ring = TpRing(net, attended, gathered)
    ring.cross()
    for step in (1, 2, 3, 4):
        ring.step(step)
    ring.finish()
    load.wait()
    block[...] = jnp.zeros_like(block)

    def add(b, _):
        block[...] += jnp.dot(gathered[b], rows_here[b], preferred_element_type=jnp.float32)
        return 0

    lax.fori_loop(0, 16, add, 0)
    net.drain()
    assert len(net.copies) <= BACK_COPIES


def back(attended, out_rows):
    rows, cols = attended.shape
    vmem = pl.BlockSpec(memory_space=pltpu.VMEM)
    return pl.pallas_call(
        back_kernel,
        out_shape=jax.ShapeDtypeStruct((rows, out_rows.shape[2]), jnp.float32),
        in_specs=[vmem, pl.BlockSpec(memory_space=pl.ANY)],
        out_specs=vmem,
        scratch_shapes=[
            pltpu.VMEM((16, rows, cols), jnp.bfloat16),
            pltpu.VMEM(out_rows.shape, jnp.bfloat16),
            pltpu.SemaphoreType.DMA((1,)),
            pltpu.SemaphoreType.DMA((BACK_COPIES,)),
            pltpu.SemaphoreType.DMA((BACK_COPIES,)),
        ],
        compiler_params=pltpu.CompilerParams(
            collective_id=1, has_side_effects=True, vmem_limit_bytes=30 << 20
        ),
        name="back",
    )(attended, out_rows)


def per_device(
    stream,
    pending,
    norm_gain,
    w_query,
    w_key,
    w_value,
    w_out,
    prefix_keys,
    prefix_values,
    prefix_segments,
    stretch_segments,
    stretch_offset,
):
    rows, cols = stream.shape
    z, xl = lax.axis_index("tp") // 2, lax.axis_index("tp") % 2
    carried = lax.psum_scatter(pending[0], "tp", scatter_dimension=1, tiled=True)

    token = lax.axis_index("ctx") * rows + jnp.arange(rows, dtype=jnp.int32)
    positions = stretch_offset[0].astype(jnp.float32) + token.astype(jnp.float32)
    angles = positions[:, None] * inverse_freqs(HD)
    cos, sin = jnp.cos(angles), jnp.sin(angles)
    cosine = jnp.concatenate([cos, cos], axis=1)
    sinus = jnp.concatenate([-sin, sin], axis=1)

    key_cols = lax.dynamic_slice_in_dim(w_key, z * HD, HD, 1)
    value_cols = lax.dynamic_slice_in_dim(w_value, z * HD, HD, 1)
    weight = jnp.concatenate([w_query, jnp.where(xl == 0, key_cols, value_cols)], axis=1)
    labels = jnp.concatenate([prefix_segments, stretch_segments]).reshape(-1, HD)
    labels = jnp.pad(labels, ((0, LABEL_ROWS - labels.shape[0]), (0, 0))).astype(jnp.bfloat16)
    old = jnp.concatenate(
        [
            lax.dynamic_index_in_dim(prefix_keys, z, 0, keepdims=False),
            lax.dynamic_index_in_dim(prefix_values, z, 0, keepdims=False),
            labels,
        ]
    )
    gain = norm_gain.astype(jnp.float32).reshape(16, 1, cols)
    query, cache, fresh, out_rows = front(stream, weight, old, w_out, gain, cosine, sinus)
    q_marks = stretch_segments.astype(jnp.float32)[:, None]
    attended = attend(query, fresh, q_marks, cache)
    heads = back(attended, out_rows)
    return (stream.astype(jnp.float32) + (heads + carried.astype(jnp.float32))).astype(jnp.bfloat16)


def solution(mesh):
    in_specs = (
        P("ctx", "tp"),
        P("tp", "ctx", None),
        P(),
        P("ctx", "tp"),
        P("ctx", None),
        P("ctx", None),
        P("tp", "ctx"),
        P(None, "ctx", None),
        P(None, "ctx", None),
        P("ctx"),
        P("ctx"),
        P(),
    )
    return jax.shard_map(
        per_device, mesh=mesh, in_specs=in_specs, out_specs=P("ctx", "tp"), check_vma=False
    )
```

time: 764 us -> 303 us (0.40)
  waiting for transfers between devices: 584 us -> 0.72 us
  Pallas kernels: 0 us -> 280 us
  matrix products: 88.3 us -> 0 us
  other arithmetic: 49.1 us -> 3.98 us
  blocking collectives: 22.4 us -> 0 us
    all_gather x6 -> x0, waiting for transfers between devices: 343 us -> none  [the longest x1 140 us: per_device(): whole = lax.all_gather(stream, 'tp', axis=1, tiled=True).astype(jnp.float32)]
    pallas_call x0 -> x3, Pallas kernels: none -> 280 us  [the longest x1 215 us: front(): pl.pallas_call(front_kernel, out_shape=(jax.ShapeDtypeStruct((2, rows, HD...]
    reduce_scatter x2 -> x1, waiting for transfers between devices: 239 us -> 0.02 us  [per_device(): lax.psum_scatter(pending[0], 'tp', scatter_dimension=1, tiled=True)]
    dot_general x6 -> x0, matrix products: 88.3 us -> none  [the longest x1 34.2 us: update(): jnp.einsum('hrn,hnd->hrd', weights.astype(jnp.bfloat16), value_block, pre...]
    reduce_sum x2 -> x0, other arithmetic: 43.7 us -> none  [the longest x1 39.6 us: update(): totals = jnp.sum(weights, axis=2)]
    all_gather x1 -> x0, blocking collectives: 22.4 us -> none  [per_device(): lax.all_gather(key_labels[None, None, :], 'ctx', axis=2, tiled=True)]
  transfers between devices with their start and end apart: 8 -> 1, of which waited for: 7 -> 0; matrix products, arithmetic and copies ran while one was open for 18% -> 1% of each run, Pallas kernels for 0% -> 93%
where the time goes in v1:
time: 303 us; the launch traced here: 300 us
  Pallas kernels  280 us (92%)
  between operations  14.3 us (5%)
  other arithmetic  3.98 us (1%)
    pallas_call x1, Pallas kernels, front(): pl.pallas_call(front_kernel, out_shape=(jax.ShapeDtypeStruct((2, rows, HD...  215 us
    pallas_call x1, Pallas kernels, back(): pl.pallas_call(back_kernel, out_shape=jax.ShapeDtypeStruct((rows, out_row...  35.1 us
    pallas_call x1, Pallas kernels, attend(): pl.pallas_call(attend_kernel, grid=(16,), out_shape=jax.ShapeDtypeStruct(...  29.4 us
  transfers between devices with their start and end apart: 1, of which 0 were waited for; matrix products, arithmetic and copies ran while one was open for 1% of the time, Pallas kernels for 93%

profile of v1, /device:TPU:4, one launch (start us, length us, event | category | flops | bytes accessed | tf_op | source)
XLA Modules:
  0.0 300.0 jit_solution(1040127215476134024)
XLA Ops:
  6.5 0.0 reduce-scatter.2.cloned.1.call-start
  6.5 0.0 copy-start.4
  6.5 0.0 copy-start.3
  6.5 0.0 copy-start.5
  6.5 0.0 copy-start.2
  6.5 0.7 reduce-scatter.2.cloned.1.call-update
  7.3 0.0 copy-done.4
  8.0 0.0 copy-done.3
  8.0 0.0 copy-done.5
  8.0 0.1 broadcast_in_dim.6.q_marks
  8.2 1.0 dynamic-slice_select_fusion
  9.2 0.0 copy-done.2
  9.3 0.0 copy-start
  9.3 0.0 copy-start.1
  9.3 1.1 dynamic-slice_bitcast_fusion
  10.4 0.8 fusion.2
  11.2 0.2 pad_maximum_fusion.1
  11.4 0.0 copy-done
  11.4 0.0 copy-done.1
  11.4 215.3 %front.1 = (bf16[2,384,128]{2,1,0:T(8,128)(2,1)S(1)}, bf16[16,1552,128]{2,1,0:T(8,128)(2,1)S(1)}, bf16[2,3,384,128]{3,2,1,0:T(8,128)(2,1)S(1)}, bf16[16,256,512]{2,1,0:T(8,128)(2,1)S(1)}) custom-call(bf16[384,512]{1,0:T(8,128)(2,1)S(1)} %copy-done, bf16[512,384]{1,0:T(8,128)(2,1)S(1)} %pad_maximum_fusion.weight, bf16[1552,128]{1,0:T(8,128)(2,1)S(1)} %fusion.1.old, ...), custom_call_target="tpu_custom_call" | custom-call | tf_op jit(solution)/shard_map/front/pallas_call | solution.py:348
  226.7 29.4 %attend.1.attended = bf16[384,256]{1,0:T(8,128)(2,1)S(1)} custom-call(bf16[2,384,128]{2,1,0:T(8,128)(2,1)S(1)} %get-tuple-element.9.query, bf16[2,3,384,128]{3,2,1,0:T(8,128)(2,1)S(1)} %get-tuple-element.10.fresh, bf16[16,1552,128]{2,1,0:T(8,128)(2,1)S(1)} %get-tuple-element.11.marks.old, f32[384,1]{1,0:T(8,128)S(1)} %broadcast_in_dim.6.q_marks, ...), custom_call_target="tpu_custom_call" | custom-call | flops 5284823040 | bytes 7340032 | tf_op jit(solution)/shard_map/attend/pallas_call | solution.py:438
  256.1 35.1 %back.1 = f32[384,512]{1,0:T(8,128)S(1)} custom-call(bf16[384,256]{1,0:T(8,128)(2,1)S(1)} %attend.1.attended, bf16[16,256,512]{2,1,0:T(8,128)(2,1)S(1)} %get-tuple-element.12.out_rows), custom_call_target="tpu_custom_call" | custom-call | tf_op jit(solution)/shard_map/back/pallas_call | solution.py:491
  291.2 0.0 reduce-scatter.2.cloned.1.call-done
  291.2 1.9 add_convert_fusion
  (8 shorter events, 0.1 us)
Async XLA Ops:
  6.5 284.7 %reduce-scatter.2.cloned.1.call-start = ((), (), s32[]{:S(2)}) async-start(), calls=%async_computation.1 | async-start | bytes 6684672 | tf_op jit(solution)/shard_map/reduce_scatter | solution.py:526
  6.5 0.7 copy-start.4
  6.5 1.4 copy-start.3
  6.5 1.4 copy-start.5
  6.5 2.7 copy-start.2
  9.3 2.1 copy-start
  9.3 2.1 copy-start.1
Sparse Core Ops, SparseCore 0:
  9.9 209.8 reduce-scatter.1

commit v2 on v1

v2 whole, which is shorter than its diff:
```python
import functools
import math

import jax
import jax.numpy as jnp
from jax import lax
from jax.experimental import pallas as pl
from jax.experimental.pallas import tpu as pltpu
from jax.sharding import PartitionSpec as P

MESH = pl.DeviceIdType.MESH
HD = 128
ROPE_BASE = 500000.0
ROPE_FACTOR = 8.0
LOW_FREQ = 1.0
HIGH_FREQ = 4.0
INITIAL_SPAN = 8192.0
NORM_EPSILON = 1e-05
MASKED = -1e30
LABEL_ROWS = 16


def inverse_freqs(head_width):
    pair_index = jnp.arange(head_width // 2, dtype=jnp.float32)
    base_freq = ROPE_BASE ** (-2.0 * pair_index / head_width)
    wavelength = 2.0 * math.pi / base_freq
    smooth = (INITIAL_SPAN / wavelength - LOW_FREQ) / (HIGH_FREQ - LOW_FREQ)
    blended = (1.0 - smooth) * base_freq / ROPE_FACTOR + smooth * base_freq
    return jnp.where(
        wavelength < INITIAL_SPAN / HIGH_FREQ,
        base_freq,
        jnp.where(wavelength > INITIAL_SPAN / LOW_FREQ, base_freq / ROPE_FACTOR, blended),
    )


def coords():
    c = lax.axis_index("ctx")
    t = lax.axis_index("tp")
    return c // 4, (c // 2) % 2, c % 2, t // 2, t % 2


def ctx_of(y, xh, core):
    return (y * 2 + xh) * 2 + core


def tp_of(z, xl):
    return z * 2 + xl


def neighbours():
    y, xh, core, z, xl = coords()
    here = ctx_of(y, xh, core)
    mine = tp_of(z, xl)
    return {
        "z+": (here, tp_of((z + 1) % 8, xl)),
        "z-": (here, tp_of((z + 7) % 8, xl)),
        "xl": (here, tp_of(z, 1 - xl)),
        "y+": (ctx_of((y + 1) % 4, xh, core), mine),
        "y-": (ctx_of((y + 3) % 4, xh, core), mine),
        "xh": (ctx_of(y, 1 - xh, core), mine),
        "xd": (ctx_of(y, 1 - xh, core), tp_of(z, 1 - xl)),
        "sib": (ctx_of(y, xh, 1 - core), mine),
    }


def greet(devices):
    barrier = pltpu.get_barrier_semaphore()
    for device in devices:
        pl.semaphore_signal(barrier, inc=1, device_id=device, device_id_type=MESH)
    pl.semaphore_wait(barrier, len(devices))


class Copy:
    def __init__(self, net, k, ref, device):
        self.root, self.shape = getattr(ref, "ref", ref), ref.shape
        self.net, self.k, self.device = net, k, device

    def handle(self):
        lead = (0,) * (len(self.root.shape) - len(self.shape))
        like = self.root.at[(*lead, *(pl.ds(0, n) for n in self.shape))]
        return pltpu.make_async_remote_copy(
            src_ref=like,
            dst_ref=like,
            send_sem=self.net.send_sem.at[self.k],
            recv_sem=self.net.recv_sem.at[self.k],
            device_id=self.device,
            device_id_type=MESH,
        )

    def wait_recv(self):
        self.handle().wait_recv()

    def wait_send(self):
        self.handle().wait_send()


class Net:
    def __init__(self, links, send_sem, recv_sem):
        self.links, self.send_sem, self.recv_sem = links, send_sem, recv_sem
        self.copies = []

    def push(self, src, link, dst=None):
        k = len(self.copies)
        device = self.links[link] if isinstance(link, str) else link
        pltpu.make_async_remote_copy(
            src_ref=src,
            dst_ref=src if dst is None else dst,
            send_sem=self.send_sem.at[k],
            recv_sem=self.recv_sem.at[k],
            device_id=device,
            device_id_type=MESH,
        ).start()
        self.copies.append(Copy(self, k, src, device))
        return self.copies[-1]

    def drain(self):
        for copy in self.copies:
            copy.wait_send()


class TpRing:
    def __init__(self, net, own, buf):
        self.net, self.buf = net, buf
        rows = own.shape[0]
        half, quarter = rows // 2, rows // 4
        self.low, self.high = pl.ds(0, half), pl.ds(half, half)
        self.parts = (pl.ds(half, quarter), pl.ds(half + quarter, quarter))
        _, _, _, z, xl = coords()
        t = tp_of(z, xl)
        self.swap = net.push(own.at[self.low], "xl", buf.at[t, self.low])
        self.hop = {}
        for way in ("z+", "z-"):
            self.hop[way, "own"] = net.push(own.at[self.low], way, buf.at[t, self.low])
            self.hop[way, "high"] = net.push(own.at[self.high], way, buf.at[t, self.high])
        self.across = [net.push(own.at[self.high], "xl", buf.at[t, self.high])]

    def cross(self):
        _, _, _, z, xl = coords()
        self.swap.wait_recv()
        for way in ("z+", "z-"):
            self.hop[way, "other"] = self.net.push(self.buf.at[tp_of(z, 1 - xl), self.low], way)

    def step(self, step):
        _, _, _, z, xl = coords()
        push, buf, hop = self.net.push, self.buf, self.hop
        for way, sign in (("z+", -1), ("z-", 1)):
            at = (z + sign * step + 8) % 8
            mine, theirs = tp_of(at, xl), tp_of(at, 1 - xl)
            part = 0 if way == "z+" else 1
            if step < 4:
                hop[way, "own"].wait_recv()
                if step < 3 or part == 0:
                    hop[way, "own"] = push(buf.at[mine, self.low], way)
                hop[way, "high"].wait_recv()
                rows = self.high if step < 3 else self.parts[part]
                hop[way, "high"] = push(buf.at[mine, rows], way)
                self.across.append(push(buf.at[mine, self.high], "xl"))
                hop[way, "other"].wait_recv()
                if step < 3 or part == 1:
                    hop[way, "other"] = push(buf.at[theirs, self.low], way)
            else:
                hop[way, "own" if part == 0 else "other"].wait_recv()
                hop[way, "high"].wait_recv()
                self.across.append(push(buf.at[mine, self.parts[part]], "xl"))

    def finish(self):
        for copy in self.across:
            copy.wait_recv()


class CtxRing:
    def __init__(self, net, own, buf, side_link):
        self.net, self.own, self.buf = net, own, buf
        y, xh, core, _, _ = coords()
        self.c, self.beside = ctx_of(y, xh, core), ctx_of(y, 1 - xh, core)
        self.side = net.push(own, side_link, buf.at[self.c])
        self.sib = [net.push(own, "sib", buf.at[self.c])]
        self.hop = {}

    def send_own(self):
        for way in ("y+", "y-"):
            self.hop[way, "own"] = self.net.push(self.own, way, self.buf.at[self.c])

    def send_side(self):
        self.side.wait_recv()
        for way in ("y+", "y-"):
            self.hop[way, "side"] = self.net.push(self.buf.at[self.beside], way)
        self.sib.append(self.net.push(self.buf.at[self.beside], "sib"))

    def step(self, step):
        y, xh, core, _, _ = coords()
        push, buf, hop = self.net.push, self.buf, self.hop
        for way, sign in (("y+", -1), ("y-", 1)):
            at = (y + sign * step + 4) % 4
            own, beside = ctx_of(at, xh, core), ctx_of(at, 1 - xh, core)
            first = way == "y+"
            if step == 1:
                hop[way, "own"].wait_recv()
                if first:
                    hop[way, "own"] = push(buf.at[own], way)
                self.sib.append(push(buf.at[own], "sib"))
                hop[way, "side"].wait_recv()
                if not first:
                    hop[way, "side"] = push(buf.at[beside], way)
                self.sib.append(push(buf.at[beside], "sib"))
            else:
                hop[way, "own" if first else "side"].wait_recv()
                self.sib.append(push(buf.at[own if first else beside], "sib"))

    def finish(self):
        for copy in self.sib:
            copy.wait_recv()


class PendingSum:
    def __init__(self, net, pending, slabs, crossed, landed, landed_parts, final, sems):
        self.net, self.slabs, self.crossed = net, slabs, crossed
        self.landed, self.landed_parts, self.final = landed, landed_parts, final
        _, _, _, self.z, self.xl = coords()
        rows, cols = slabs.shape[1:]
        half, quarter = rows // 2, rows // 4
        self.low, self.high = pl.ds(0, half), pl.ds(half, half)
        self.parts = (pl.ds(half, quarter), pl.ds(half + quarter, quarter))
        self.loads = [
            pltpu.make_async_copy(
                pending.at[0, :, pl.ds(k * cols, cols)], slabs.at[k], sems.at[k]
            )
            for k in range(16)
        ]
        for load in self.loads:
            load.start()
        self.hop = {}

    def at(self, offset, other=0):
        return tp_of((self.z + offset + 8) % 8, (self.xl + other) % 2)

    def cross(self):
        for load in self.loads:
            load.wait()
        self.over = {}
        for offset in (4, 3, -3, 2, -2, 1, -1, 0):
            slot = (self.z + offset + 8) % 8
            self.over[offset] = self.net.push(
                self.slabs.at[self.at(offset, 1), self.high], "xl", self.crossed.at[slot]
            )

    def add(self, index, rows, more):
        total = self.slabs[index, rows].astype(jnp.float32) + more.astype(jnp.float32)
        self.slabs[index, rows] = total.astype(jnp.bfloat16)

    def take_crossed(self, offset):
        self.over[offset].wait_recv()
        slot = (self.z + offset + 8) % 8
        self.add(self.at(offset), self.high, self.crossed[slot])

    def land(self, way, kind, step):
        if kind == 2 and step == 0:
            return self.landed_parts.at[way]
        return self.landed.at[way, kind, step]

    def send(self, way, kind, step, index, rows):
        self.hop[way, kind] = self.net.push(
            self.slabs.at[index, rows], ("z+", "z-")[way], self.land(way, kind, step)
        )

    def first(self):
        self.send(0, 0, 0, self.at(4), self.low)
        self.send(1, 1, 0, self.at(4, 1), self.low)

    def first_high(self):
        self.take_crossed(4)
        for way in (0, 1):
            self.send(way, 2, 0, self.at(4), self.parts[way])

    def step(self, step):
        for way, sign in ((0, 1), (1, -1)):
            offset = sign * (4 - step)
            for kind in (0, 1, 2):
                index = self.at(offset, 1 if kind == 1 else 0)
                rows = self.high if kind == 2 else self.low
                if kind == 2:
                    self.take_crossed(offset)
                if step > 1 or kind == 2 or kind == way:
                    self.hop[way, kind].wait_recv()
                    into = self.parts[way] if kind == 2 and step == 1 else rows
                    self.add(index, into, self.land(way, kind, step - 1)[...])
                self.send(way, kind, step, index, rows)

    def last_other(self):
        for way in (0, 1):
            self.hop[way, 1].wait_recv()
        more = self.landed[0, 1, 3].astype(jnp.float32) + self.landed[1, 1, 3].astype(jnp.float32)
        self.add(self.at(0, 1), self.low, more)
        self.fold = self.net.push(self.slabs.at[self.at(0, 1), self.low], "xl", self.final)

    def last(self):
        wide = jnp.float32
        for way in (0, 1):
            self.hop[way, 0].wait_recv()
            self.hop[way, 2].wait_recv()
        self.over[0].wait_recv()
        self.fold.wait_recv()
        low = self.slabs[self.at(0), self.low].astype(wide) + self.final[...].astype(wide)
        low = low + self.landed[0, 0, 3].astype(wide) + self.landed[1, 0, 3].astype(wide)
        high = self.slabs[self.at(0), self.high].astype(wide) + self.crossed[self.z].astype(wide)
        high = high + self.landed[0, 2, 3].astype(wide) + self.landed[1, 2, 3].astype(wide)
        return low, high


COPIES = 208


def block_kernel(
    stream, pending, w_query, w_key, w_value, w_out, old_keys, old_values, labels,
    gain, cosine, sinus, q_marks,
    output,
    blocks, weights, cache, out_rows, gathered,
    slabs, crossed, landed, landed_parts, final,
    totals, squares, query, made, fresh, turned, attended, total_out,
    top, total, mix,
    local_sem, load_sem, send_sem, recv_sem, turn_sem,
):
    y, xh, core, z, xl = coords()
    c, t = ctx_of(y, xh, core), tp_of(z, xl)
    rows = stream.shape[0]
    span = old_keys.shape[1]
    q_cols = w_query.shape[1]
    heads = q_cols // HD

    local = [
        pltpu.make_async_copy(stream, blocks.at[t], local_sem.at[0]),
        pltpu.make_async_copy(w_query, weights.at[c, :, pl.ds(0, q_cols)], local_sem.at[1]),
        pltpu.make_async_copy(old_keys.at[z], cache.at[c, pl.ds(0, span)], local_sem.at[2]),
        pltpu.make_async_copy(old_values.at[z], cache.at[c, pl.ds(span, span)], local_sem.at[3]),
        pltpu.make_async_copy(labels, cache.at[c, pl.ds(2 * span, LABEL_ROWS)], local_sem.at[4]),
    ]
    head_cols = pl.ds(pl.multiple_of(z * HD, HD), HD)
    kv_slot = weights.at[c, :, pl.ds(q_cols, HD)]
    key_copy = pltpu.make_async_copy(w_key.at[:, head_cols], kv_slot, local_sem.at[5])
    value_copy = pltpu.make_async_copy(w_value.at[:, head_cols], kv_slot, local_sem.at[5])
    for copy in local:
        copy.start()

    @pl.when(xl == 0)
    def _():
        key_copy.start()

    @pl.when(xl == 1)
    def _():
        value_copy.start()

    links = neighbours()
    later = {}
    for ahead in (1, 2):
        for other in (0, 1):
            later[ahead, other] = ((c + ahead) % 16, tp_of(z, (xl + other) % 2))
    earlier = [
        ((c + 16 - ahead) % 16, tp_of(z, (xl + other) % 2)) for ahead in (1, 2) for other in (0, 1)
    ]
    peers = list(links.values()) + list(later.values()) + earlier
    barrier = pltpu.get_barrier_semaphore()
    for device in peers:
        pl.semaphore_signal(barrier, inc=1, device_id=device, device_id_type=MESH)

    @pl.when(c != t)
    def _():
        pl.semaphore_signal(barrier, inc=1, device_id=(t, c), device_id_type=MESH)
        pl.semaphore_wait(barrier, len(peers) + 1)

    @pl.when(c == t)
    def _():
        pl.semaphore_wait(barrier, len(peers))

    net = Net(links, send_sem, recv_sem)
    tp_ring = TpRing(net, stream, blocks)
    local[1].wait()
    key_copy.wait()
    w_ring = CtxRing(net, weights.at[c], weights, "xh")
    w_ring.send_own()
    for k in (2, 3, 4):
        local[k].wait()
    old_ring = CtxRing(net, cache.at[c], cache, "xd")

    turn = pltpu.make_async_remote_copy(
        src_ref=w_out,
        dst_ref=turned,
        send_sem=turn_sem.at[0],
        recv_sem=turn_sem.at[1],
        device_id=(t, c),
        device_id_type=MESH,
    )
    stay = pltpu.make_async_copy(w_out, turned, turn_sem.at[2])

    @pl.when(c != t)
    def _():
        turn.start()

    @pl.when(c == t)
    def _():
        stay.start()

    sums = PendingSum(net, pending, slabs, crossed, landed, landed_parts, final, load_sem)
    tp_ring.cross()
    w_ring.send_side()
    tp_ring.step(1)
    w_ring.step(1)
    old_ring.send_own()
    old_ring.send_side()
    tp_ring.step(2)
    w_ring.step(2)
    tp_ring.step(3)
    old_ring.step(1)

    @pl.when(c != t)
    def _():
        turn.wait_send()
        turn.wait_recv()

    @pl.when(c == t)
    def _():
        stay.wait()

    out_ring = CtxRing(net, turned, out_rows, "xh")
    out_ring.send_own()
    own_out = pltpu.make_async_copy(turned, out_rows.at[c], local_sem.at[6])
    own_out.start()
    tp_ring.step(4)
    sums.cross()
    sums.first()
    w_ring.finish()
    tp_ring.finish()
    local[0].wait()

    totals[...] = jnp.zeros_like(totals)
    squares[...] = jnp.zeros_like(squares)

    def project(b, _):
        wide = blocks[b].astype(jnp.float32)
        part = wide * wide
        squares[...] += sum(part[:, k * HD : (k + 1) * HD] for k in range(part.shape[1] // HD))
        low = (wide * gain[b]).astype(jnp.bfloat16)
        totals[...] += jnp.dot(low, weights[b], preferred_element_type=jnp.float32)
        return 0

    lax.fori_loop(0, 8, project, 0)
    sums.first_high()
    out_ring.send_side()
    lax.fori_loop(8, 16, project, 0)
    width = 16 * stream.shape[1]
    mean_square = jnp.sum(squares[...], axis=1, keepdims=True) / width
    scale = lax.rsqrt(mean_square + NORM_EPSILON)
    cos, sin = cosine[...], sinus[...]

    def rotate(part):
        return part * cos + pltpu.roll(part, HD // 2, 1) * sin

    part = totals[:, 2 * HD :] * scale

    @pl.when(xl == 0)
    def _():
        made[...] = rotate(part).astype(jnp.bfloat16)

    @pl.when(xl == 1)
    def _():
        made[...] = part.astype(jnp.bfloat16)

    keep = pltpu.make_async_copy(made, fresh.at[xl, 2], local_sem.at[7])
    keep.start()
    sent = [net.push(made, "xl", fresh.at[xl, 2])]
    for (ahead, _), device in later.items():
        sent.append(net.push(made, device, fresh.at[xl, 2 - ahead]))
    sums.step(1)

    to_exponent = math.log2(math.e) / math.sqrt(HD)
    for h in range(heads):
        part = totals[:, h * HD : (h + 1) * HD] * scale
        query[h] = (rotate(part) * to_exponent).astype(jnp.bfloat16)

    top[...] = jnp.full_like(top, MASKED)
    total[...] = jnp.zeros_like(total)
    mix[...] = jnp.zeros_like(mix)
    own_marks = q_marks[...]

    def absorb(h, keys, values, seen):
        scores = lax.dot_general(
            query[h], keys, (((1,), (1,)), ((), ())), preferred_element_type=jnp.float32
        )
        scores = jnp.where(seen, scores, MASKED)
        before = top[h]
        now = jnp.maximum(before, jnp.max(scores, axis=1, keepdims=True))
        fade = jnp.exp2(before - now)
        shares = jnp.exp2(scores - now[:, :1])
        total[h] = total[h] * fade + jnp.sum(shares, axis=1, keepdims=True)
        mix[h] = mix[h] * fade + jnp.dot(
            shares.astype(jnp.bfloat16), values, preferred_element_type=jnp.float32
        )
        top[h] = now

    def row_of(marks, first, count):
        wide = marks.astype(jnp.float32)
        return jnp.concatenate([wide[first + k : first + k + 1] for k in range(count)], axis=1)

    def over_prefix(i, _):
        def on(k, *actions):
            @pl.when(i == k)
            def _():
                for action in actions:
                    action()

        for k in range(16):
            if k in before_block:
                on(k, *before_block[k])
        group = i // 4
        turn_y = jnp.where(group == 1, 3, jnp.where(group == 2, 1, jnp.where(group == 3, 2, 0)))
        at = ctx_of((y + turn_y) % 4, (xh + (i // 2) % 2) % 2, (core + i % 2) % 2)
        marks = row_of(cache[at, 2 * span :], 0, span // HD)
        seen = marks <= own_marks
        for h in range(heads):
            absorb(h, cache[at, :span], cache[at, span : 2 * span], seen)
        return 0

    def sib(ring, *numbers):
        def wait():
            for k in numbers:
                ring.sib[k].wait_recv()

        return wait

    before_block = {
        0: [sib(old_ring, 0, 1)],
        2: [lambda: old_ring.step(2), lambda: out_ring.step(1)],
        4: [sib(old_ring, 2, 3)],
        6: [lambda: sums.step(2)],
        8: [sib(old_ring, 4, 5), lambda: out_ring.step(2)],
        12: [sib(old_ring, 6, 7)],
        13: [lambda: sums.step(3)],
    }
    lax.fori_loop(0, 16, over_prefix, 0)
    for copy in sent:
        copy.wait_recv()
    keep.wait()
    for j in range(3):
        back = 2 - j
        row = row_of(cache[(c + 16 - back) % 16, 2 * span :], span // HD, rows // HD)
        row = jnp.where(c >= back, row, -1.0)
        same = row == own_marks
        if back == 0:
            at = lax.broadcasted_iota(jnp.int32, (rows, rows), 0)
            key_at = lax.broadcasted_iota(jnp.int32, (rows, rows), 1)
            same = same & (key_at <= at)
        for h in range(heads):
            absorb(h, fresh[0, j], fresh[1, j], same)
    for h in range(heads):
        attended[:, h * HD : (h + 1) * HD] = (mix[h] / total[h]).astype(jnp.bfloat16)

    ring = TpRing(net, attended, gathered)
    gathered[t] = attended[...]
    sums.last_other()
    out_ring.finish()
    own_out.wait()
    ring.cross()
    for step in (1, 2, 3, 4):
        ring.step(step)
    low, high = sums.last()
    half = rows // 2
    total_out[:half] = low
    total_out[half:] = high
    ring.finish()

    def project_out(b, _):
        total_out[...] += jnp.dot(gathered[b], out_rows[b], preferred_element_type=jnp.float32)
        return 0

    lax.fori_loop(0, 16, project_out, 0)
    output[...] = (blocks[t].astype(jnp.float32) + total_out[...]).astype(jnp.bfloat16)
    net.drain()
    assert len(net.copies) <= COPIES


def run_block(stream, pending, w_query, w_key, w_value, w_out, old_keys, old_values, labels,
              gain, cosine, sinus, q_marks):
    rows, cols = stream.shape
    depth, q_cols = w_query.shape
    span = old_keys.shape[1]
    low, wide = jnp.bfloat16, jnp.float32
    half = rows // 2
    any_spec = pl.BlockSpec(memory_space=pl.ANY)
    vmem = pl.BlockSpec(memory_space=pltpu.VMEM)
    heads = q_cols // HD
    return pl.pallas_call(
        block_kernel,
        out_shape=jax.ShapeDtypeStruct((rows, cols), low),
        in_specs=[any_spec] * 9 + [vmem] * 4,
        out_specs=vmem,
        scratch_shapes=[
            pltpu.VMEM((16, rows, cols), low),
            pltpu.VMEM((16, depth, q_cols + HD), low),
            pltpu.VMEM((16, 2 * span + LABEL_ROWS, HD), low),
            pltpu.VMEM((16, *w_out.shape), low),
            pltpu.VMEM((16, rows, q_cols), low),
            pltpu.VMEM((16, rows, cols), low),
            pltpu.VMEM((8, half, cols), low),
            pltpu.VMEM((2, 3, 4, half, cols), low),
            pltpu.VMEM((2, half // 2, cols), low),
            pltpu.VMEM((half, cols), low),
            pltpu.VMEM((rows, q_cols + HD), wide),
            pltpu.VMEM((rows, HD), wide),
            pltpu.VMEM((heads, rows, HD), low),
            pltpu.VMEM((rows, HD), low),
            pltpu.VMEM((2, 3, rows, HD), low),
            pltpu.VMEM(w_out.shape, low),
            pltpu.VMEM((rows, q_cols), low),
            pltpu.VMEM((rows, cols), wide),
            pltpu.VMEM((heads, rows, HD), wide),
            pltpu.VMEM((heads, rows, HD), wide),
            pltpu.VMEM((heads, rows, HD), wide),
            pltpu.SemaphoreType.DMA((8,)),
            pltpu.SemaphoreType.DMA((16,)),
            pltpu.SemaphoreType.DMA((COPIES,)),
            pltpu.SemaphoreType.DMA((COPIES,)),
            pltpu.SemaphoreType.DMA((3,)),
        ],
        compiler_params=pltpu.CompilerParams(
            collective_id=0, has_side_effects=True, vmem_limit_bytes=58 << 20
        ),
        name="attention_block",
    )(stream, pending, w_query, w_key, w_value, w_out, old_keys, old_values, labels,
      gain, cosine, sinus, q_marks)


def per_device(
    stream,
    pending,
    norm_gain,
    w_query,
    w_key,
    w_value,
    w_out,
    prefix_keys,
    prefix_values,
    prefix_segments,
    stretch_segments,
    stretch_offset,
):
    rows, cols = stream.shape
    token = lax.axis_index("ctx") * rows + jnp.arange(rows, dtype=jnp.int32)
    positions = stretch_offset[0].astype(jnp.float32) + token.astype(jnp.float32)
    angles = positions[:, None] * inverse_freqs(HD)
    cos, sin = jnp.cos(angles), jnp.sin(angles)
    cosine = jnp.concatenate([cos, cos], axis=1)
    sinus = jnp.concatenate([-sin, sin], axis=1)
    labels = jnp.concatenate([prefix_segments, stretch_segments]).reshape(-1, HD)
    labels = jnp.pad(labels, ((0, LABEL_ROWS - labels.shape[0]), (0, 0))).astype(jnp.bfloat16)
    gain = norm_gain.astype(jnp.float32).reshape(16, 1, cols)
    q_marks = stretch_segments.astype(jnp.float32)[:, None]
    return run_block(
        stream, pending, w_query, w_key, w_value, w_out, prefix_keys, prefix_values, labels,
        gain, cosine, sinus, q_marks,
    )


def solution(mesh):
    in_specs = (
        P("ctx", "tp"),
        P("tp", "ctx", None),
        P(),
        P("ctx", "tp"),
        P("ctx", None),
        P("ctx", None),
        P("tp", "ctx"),
        P(None, "ctx", None),
        P(None, "ctx", None),
        P("ctx"),
        P("ctx"),
        P(),
    )
    return jax.shard_map(
        per_device, mesh=mesh, in_specs=in_specs, out_specs=P("ctx", "tp"), check_vma=False
    )
```

time: 303 us -> 192 us (0.63)
  Pallas kernels: 280 us -> 185 us
  between operations: 14.3 us -> 0.72 us
    pallas_call x3 -> x1, Pallas kernels: 280 us -> 185 us  [run_block(): pl.pallas_call(block_kernel, out_shape=jax.ShapeDtypeStruct((rows, cols),...]
  transfers between devices with their start and end apart: 1 -> 0, of which waited for: 0 -> 0; matrix products, arithmetic and copies ran while one was open for 1% -> 0% of each run, Pallas kernels for 93% -> 0%
where the time goes in v2:
time: 192 us
  Pallas kernels  185 us (96%)
  local copies, waits for them, and re-layouts  3.16 us (2%)
  other arithmetic  2.35 us (1%)
    pallas_call x1, Pallas kernels, run_block(): pl.pallas_call(block_kernel, out_shape=jax.ShapeDtypeStruct((rows, cols),...  185 us

profile of v2, /device:TPU:4, one launch (start us, length us, event | category | flops | bytes accessed | tf_op | source)
XLA Modules:
  0.0 191.7 jit_solution(11380362821510257778)
XLA Ops:
  0.0 0.0 copy-start.2
  0.0 0.0 copy-start.1
  0.0 0.0 copy-start
  0.7 0.8 fusion
  1.5 0.9 pad_maximum_fusion
  2.4 0.0 copy-done.2
  2.4 0.8 broadcast_in_dim.6.q_marks
  3.2 0.0 copy-done.1
  3.2 0.6 pad.5.labels
  3.8 0.0 copy-done
  3.8 0.6 reshape.40
  4.5 185.5 %attention_block.1 = bf16[384,512]{1,0:T(8,128)(2,1)} custom-call(bf16[384,512]{1,0:T(8,128)(2,1)} %stream.1, bf16[1,384,8192]{2,1,0:T(8,128)(2,1)} %pending.1, bf16[512,256]{1,0:T(8,128)(2,1)} %w_query.1, bf16[512,1024]{1,0:T(8,128)(2,1)} %w_key.1, bf16[512,1024]{1,0:T(8,128)(2,1)} %w_value.1, bf16[256,512]{1,0:T(8,128)(2,1)} %w_out.1, ...), custom_call_target="tpu_custom_call" | custom-call | tf_op jit(solution)/shard_map/attention_block/pallas_call | solution.py:590
  189.9 1.8 copy.16
  (5 shorter events, 0.0 us)
Async XLA Ops:
  0.0 2.4 %copy-start.2 = (s32[384]{0:T(512)S(1)}, s32[384]{0:T(512)}, u32[]{:S(2)}) copy-start(s32[384]{0:T(512)} %param.22) | copy-start | bytes 4612
  0.0 3.2 %copy-start.1 = (s32[768]{0:T(1024)S(1)}, s32[768]{0:T(1024)}, u32[]{:S(2)}) copy-start(s32[768]{0:T(1024)} %param.21) | copy-start | bytes 9220
  0.0 3.8 %copy-start = (bf16[8192]{0:T(1024)(128)(2,1)S(1)}, bf16[8192]{0:T(1024)(128)(2,1)}, u32[]{:S(2)}) copy-start(bf16[8192]{0:T(1024)(128)(2,1)} %param.14) | copy-start | bytes 49156

commit v3 on v2

--- a/solution.py
+++ b/solution.py
@@ -119,12 +119,12 @@
 
 
 class TpRing:
-    def __init__(self, net, own, buf):
-        self.net, self.buf = net, buf
-        rows = own.shape[0]
-        half, quarter = rows // 2, rows // 4
-        self.low, self.high = pl.ds(0, half), pl.ds(half, half)
-        self.parts = (pl.ds(half, quarter), pl.ds(half + quarter, quarter))
+    def __init__(self, net, own, buf, upper):
+        self.net, self.own, self.buf = net, own, buf
+        half = own.shape[0] - upper
+        part = -(-upper // 32) * 16
+        self.low, self.high = pl.ds(0, half), pl.ds(half, upper)
+        self.parts = (pl.ds(half, part), pl.ds(half + part, upper - part))
         _, _, _, z, xl = coords()
         t = tp_of(z, xl)
         self.swap = net.push(own.at[self.low], "xl", buf.at[t, self.low])
@@ -132,83 +132,155 @@
         for way in ("z+", "z-"):
             self.hop[way, "own"] = net.push(own.at[self.low], way, buf.at[t, self.low])
             self.hop[way, "high"] = net.push(own.at[self.high], way, buf.at[t, self.high])
-        self.across = [net.push(own.at[self.high], "xl", buf.at[t, self.high])]
+        self.across = []
 
     def cross(self):
         _, _, _, z, xl = coords()
         self.swap.wait_recv()
         for way in ("z+", "z-"):
             self.hop[way, "other"] = self.net.push(self.buf.at[tp_of(z, 1 - xl), self.low], way)
+        self.across.append(
+            self.net.push(self.own.at[self.high], "xl", self.buf.at[tp_of(z, xl), self.high])
+        )
 
     def step(self, step):
         _, _, _, z, xl = coords()
         push, buf, hop = self.net.push, self.buf, self.hop
-        for way, sign in (("z+", -1), ("z-", 1)):
-            at = (z + sign * step + 8) % 8
-            mine, theirs = tp_of(at, xl), tp_of(at, 1 - xl)
-            part = 0 if way == "z+" else 1
-            if step < 4:
-                hop[way, "own"].wait_recv()
-                if step < 3 or part == 0:
-                    hop[way, "own"] = push(buf.at[mine, self.low], way)
-                hop[way, "high"].wait_recv()
-                rows = self.high if step < 3 else self.parts[part]
-                hop[way, "high"] = push(buf.at[mine, rows], way)
-                self.across.append(push(buf.at[mine, self.high], "xl"))
-                hop[way, "other"].wait_recv()
-                if step < 3 or part == 1:
-                    hop[way, "other"] = push(buf.at[theirs, self.low], way)
-            else:
-                hop[way, "own" if part == 0 else "other"].wait_recv()
-                hop[way, "high"].wait_recv()
-                self.across.append(push(buf.at[mine, self.parts[part]], "xl"))
-
-    def finish(self):
-        for copy in self.across:
+        for kind in ("own", "high", "other"):
+            for way, sign in (("z+", -1), ("z-", 1)):
+                at = (z + sign * step + 8) % 8
+                mine, theirs = tp_of(at, xl), tp_of(at, 1 - xl)
+                part = 0 if way == "z+" else 1
+                if kind == "high":
+                    hop[way, kind].wait_recv()
+                    if step < 4:
+                        rows = self.high if step < 3 else self.parts[part]
+                        hop[way, kind] = push(buf.at[mine, rows], way)
+                    rows = self.high if step < 4 else self.parts[part]
+                    self.across.append(push(buf.at[mine, rows], "xl"))
+                    continue
+                last = part == (0 if kind == "own" else 1)
+                if step < 4 or last:
+                    hop[way, kind].wait_recv()
+                if step < 3 or (step == 3 and last):
+                    hop[way, kind] = push(buf.at[mine if kind == "own" else theirs, self.low], way)
+
+    def arrive(self, first, last):
+        for copy in self.across[first:last]:
             copy.wait_recv()
 
 
 class CtxRing:
-    def __init__(self, net, own, buf, side_link):
-        self.net, self.own, self.buf = net, own, buf
+    def __init__(self, net, own, slot, side_link):
+        self.net, self.own, self.slot, self.side_link = net, own, slot, side_link
         y, xh, core, _, _ = coords()
         self.c, self.beside = ctx_of(y, xh, core), ctx_of(y, 1 - xh, core)
-        self.side = net.push(own, side_link, buf.at[self.c])
-        self.sib = [net.push(own, "sib", buf.at[self.c])]
-        self.hop = {}
+        self.sib, self.hop = [], {}
+
+    def send_across(self):
+        self.side = self.net.push(self.own, self.side_link, self.slot(self.c))
+        self.sib.append(self.net.push(self.own, "sib", self.slot(self.c)))
 
     def send_own(self):
         for way in ("y+", "y-"):
-            self.hop[way, "own"] = self.net.push(self.own, way, self.buf.at[self.c])
+            self.hop[way, "own"] = self.net.push(self.own, way, self.slot(self.c))
 
     def send_side(self):
         self.side.wait_recv()
         for way in ("y+", "y-"):
-            self.hop[way, "side"] = self.net.push(self.buf.at[self.beside], way)
-        self.sib.append(self.net.push(self.buf.at[self.beside], "sib"))
-
-    def step(self, step):
+            self.hop[way, "side"] = self.net.push(self.slot(self.beside), way)
+        self.sib.append(self.net.push(self.slot(self.beside), "sib"))
+
+    def came(self, way, step, kind):
         y, xh, core, _, _ = coords()
-        push, buf, hop = self.net.push, self.buf, self.hop
-        for way, sign in (("y+", -1), ("y-", 1)):
-            at = (y + sign * step + 4) % 4
-            own, beside = ctx_of(at, xh, core), ctx_of(at, 1 - xh, core)
-            first = way == "y+"
-            if step == 1:
-                hop[way, "own"].wait_recv()
-                if first:
-                    hop[way, "own"] = push(buf.at[own], way)
-                self.sib.append(push(buf.at[own], "sib"))
-                hop[way, "side"].wait_recv()
-                if not first:
-                    hop[way, "side"] = push(buf.at[beside], way)
-                self.sib.append(push(buf.at[beside], "sib"))
-            else:
-                hop[way, "own" if first else "side"].wait_recv()
-                self.sib.append(push(buf.at[own if first else beside], "sib"))
+        at = (y + (-step if way == "y+" else step) + 4) % 4
+        self.hop[way, kind].wait_recv()
+        return self.slot(ctx_of(at, xh if kind == "own" else 1 - xh, core))
+
+    def near(self, kind):
+        for way in ("y+", "y-"):
+            block = self.came(way, 1, kind)
+            if (way == "y+") == (kind == "own"):
+                self.hop[way, kind] = self.net.push(block, way)
+            self.sib.append(self.net.push(block, "sib"))
+
+    def far(self):
+        for way, kind in (("y+", "own"), ("y-", "side")):
+            self.sib.append(self.net.push(self.came(way, 2, kind), "sib"))
 
     def finish(self):
         for copy in self.sib:
+            copy.wait_recv()
+
+
+class Turn:
+    def __init__(self, net, w_out, mid, turned, sems):
+        self.net, self.w_out, self.mid, self.turned, self.sems = net, w_out, mid, turned, sems
+        y, xh, core, z, xl = coords()
+        self.eighth = y * 2 + xh
+        self.rows = w_out.shape[0] // 8
+        self.stays = core == xl
+
+    def place(self, ahead):
+        _, _, core, z, xl = coords()
+        at = (self.eighth + ahead) % 8
+        return (at * 2 + xl, tp_of(z, core))
+
+    def height(self, ahead):
+        _, _, _, z, xl = coords()
+        c = lax.axis_index("ctx")
+        return (c, tp_of((z + ahead) % 8, xl))
+
+    def first(self):
+        src = self.w_out.at[pl.ds(pl.multiple_of(self.eighth * self.rows, self.rows), self.rows)]
+        dst = self.mid.at[self.eighth]
+        away = pltpu.make_async_remote_copy(
+            src_ref=src,
+            dst_ref=dst,
+            send_sem=self.sems.at[0],
+            recv_sem=self.sems.at[1],
+            device_id=self.place(0),
+            device_id_type=MESH,
+        )
+        return away, pltpu.make_async_copy(src, dst, self.sems.at[2])
+
+    def spread(self):
+        away, stay = self.first()
+        pl.when(jnp.logical_not(self.stays))(away.start)
+        pl.when(self.stays)(stay.start)
+        self.got = []
+        for ahead in range(1, 8):
+            at = (self.eighth + ahead) % 8
+            src = self.w_out.at[pl.ds(pl.multiple_of(at * self.rows, self.rows), self.rows)]
+            self.got.append(self.net.push(src, self.place(ahead), self.mid.at[self.eighth]))
+
+    def own(self, z):
+        core = lax.axis_index("ctx") % 2
+        return self.turned.at[z, core, self.eighth]
+
+    def rise(self):
+        away, stay = self.first()
+
+        @pl.when(jnp.logical_not(self.stays))
+        def _():
+            away.wait_send()
+            away.wait_recv()
+
+        pl.when(self.stays)(stay.wait)
+        for copy in self.got:
+            copy.wait_recv()
+        _, _, _, z, _ = coords()
+        keep = pltpu.make_async_copy(self.mid.at[z], self.own(z), self.sems.at[3])
+        keep.start()
+        self.risen = [
+            self.net.push(self.mid.at[(z + ahead) % 8], self.height(ahead), self.own(z))
+            for ahead in range(1, 8)
+        ]
+
+    def finish(self):
+        _, _, _, z, _ = coords()
+        pltpu.make_async_copy(self.mid.at[z], self.own(z), self.sems.at[3]).wait()
+        for copy in self.risen:
             copy.wait_recv()
 
 
@@ -229,16 +301,17 @@
         ]
         for load in self.loads:
             load.start()
-        self.hop = {}
+        self.hop, self.over = {}, {}
 
     def at(self, offset, other=0):
         return tp_of((self.z + offset + 8) % 8, (self.xl + other) % 2)
 
-    def cross(self):
+    def ready(self):
         for load in self.loads:
             load.wait()
-        self.over = {}
-        for offset in (4, 3, -3, 2, -2, 1, -1, 0):
+
+    def cross(self, *offsets):
+        for offset in offsets:
             slot = (self.z + offset + 8) % 8
             self.over[offset] = self.net.push(
                 self.slabs.at[self.at(offset, 1), self.high], "xl", self.crossed.at[slot]
@@ -272,10 +345,10 @@
         for way in (0, 1):
             self.send(way, 2, 0, self.at(4), self.parts[way])
 
-    def step(self, step):
+    def step(self, step, kinds):
         for way, sign in ((0, 1), (1, -1)):
             offset = sign * (4 - step)
-            for kind in (0, 1, 2):
+            for kind in kinds:
                 index = self.at(offset, 1 if kind == 1 else 0)
                 rows = self.high if kind == 2 else self.low
                 if kind == 2:
@@ -307,16 +380,16 @@
         return low, high
 
 
-COPIES = 208
+COPIES = 256
 
 
 def block_kernel(
     stream, pending, w_query, w_key, w_value, w_out, old_keys, old_values, labels,
-    gain, cosine, sinus, q_marks,
+    gain, cosine, sinus,
     output,
     blocks, weights, cache, out_rows, gathered,
     slabs, crossed, landed, landed_parts, final,
-    totals, squares, query, made, fresh, turned, attended, total_out,
+    totals, squares, query, made, fresh, mid, attended, total_out, q_marks,
     top, total, mix,
     local_sem, load_sem, send_sem, recv_sem, turn_sem,
 ):
@@ -326,6 +399,15 @@
     span = old_keys.shape[1]
     q_cols = w_query.shape[1]
     heads = q_cols // HD
+
+    def row_of(marks, first, count):
+        wide = marks.astype(jnp.float32)
+        return jnp.concatenate([wide[first + k : first + k + 1] for k in range(count)], axis=1)
+
+    def arrival(j):
+        away = (j + 2) // 4
+        sign = 1 - 2 * (((j + 2) // 2) % 2)
+        return tp_of((z + sign * away + 8) % 8, (xl + j % 2) % 2)
 
     local = [
         pltpu.make_async_copy(stream, blocks.at[t], local_sem.at[0]),
@@ -357,84 +439,65 @@
     earlier = [
         ((c + 16 - ahead) % 16, tp_of(z, (xl + other) % 2)) for ahead in (1, 2) for other in (0, 1)
     ]
+    net = Net(links, send_sem, recv_sem)
+    turn = Turn(net, w_out, mid, out_rows, turn_sem)
     peers = list(links.values()) + list(later.values()) + earlier
+    peers += [turn.place(ahead) for ahead in range(1, 8)]
+    peers += [turn.height(ahead) for ahead in range(2, 7)]
     barrier = pltpu.get_barrier_semaphore()
     for device in peers:
         pl.semaphore_signal(barrier, inc=1, device_id=device, device_id_type=MESH)
 
-    @pl.when(c != t)
+    @pl.when(core != xl)
     def _():
-        pl.semaphore_signal(barrier, inc=1, device_id=(t, c), device_id_type=MESH)
+        pl.semaphore_signal(barrier, inc=1, device_id=turn.place(0), device_id_type=MESH)
         pl.semaphore_wait(barrier, len(peers) + 1)
 
-    @pl.when(c == t)
+    @pl.when(core == xl)
     def _():
         pl.semaphore_wait(barrier, len(peers))
 
-    net = Net(links, send_sem, recv_sem)
-    tp_ring = TpRing(net, stream, blocks)
+    tp_ring = TpRing(net, stream, blocks, 176)
     local[1].wait()
     key_copy.wait()
-    w_ring = CtxRing(net, weights.at[c], weights, "xh")
+    w_ring = CtxRing(net, weights.at[c], lambda k: weights.at[k], "xh")
     w_ring.send_own()
+    w_ring.send_across()
     for k in (2, 3, 4):
         local[k].wait()
-    old_ring = CtxRing(net, cache.at[c], cache, "xd")
-
-    turn = pltpu.make_async_remote_copy(
-        src_ref=w_out,
-        dst_ref=turned,
-        send_sem=turn_sem.at[0],
-        recv_sem=turn_sem.at[1],
-        device_id=(t, c),
-        device_id_type=MESH,
+    old_ring = CtxRing(net, cache.at[c], lambda k: cache.at[k], "xd")
+    out_ring = CtxRing(
+        net, turn.own(pl.ds(0, 8)), lambda k: out_rows.at[:, k % 2, k // 2], "xh"
     )
-    stay = pltpu.make_async_copy(w_out, turned, turn_sem.at[2])
-
-    @pl.when(c != t)
-    def _():
-        turn.start()
-
-    @pl.when(c == t)
-    def _():
-        stay.start()
-
     sums = PendingSum(net, pending, slabs, crossed, landed, landed_parts, final, load_sem)
+    row = row_of(cache[c, 2 * span :], span // HD, rows // HD)
+    flat = (rows, rows)
+    diagonal = lax.broadcasted_iota(jnp.int32, flat, 0) == lax.broadcasted_iota(jnp.int32, flat, 1)
+    q_marks[...] = jnp.sum(jnp.where(diagonal, row, 0.0), axis=1, keepdims=True) + jnp.zeros(
+        (rows, HD), jnp.float32
+    )
+    totals[...] = jnp.zeros_like(totals)
+    squares[...] = jnp.zeros_like(squares)
     tp_ring.cross()
+    turn.spread()
+    w_ring.near("own")
+    tp_ring.step(1)
     w_ring.send_side()
-    tp_ring.step(1)
-    w_ring.step(1)
+    old_ring.send_across()
+    tp_ring.step(2)
+    w_ring.near("side")
+    w_ring.far()
     old_ring.send_own()
     old_ring.send_side()
-    tp_ring.step(2)
-    w_ring.step(2)
     tp_ring.step(3)
-    old_ring.step(1)
-
-    @pl.when(c != t)
-    def _():
-        turn.wait_send()
-        turn.wait_recv()
-
-    @pl.when(c == t)
-    def _():
-        stay.wait()
-
-    out_ring = CtxRing(net, turned, out_rows, "xh")
-    out_ring.send_own()
-    own_out = pltpu.make_async_copy(turned, out_rows.at[c], local_sem.at[6])
-    own_out.start()
-    tp_ring.step(4)
-    sums.cross()
-    sums.first()
+    sums.ready()
+    sums.cross(4)
     w_ring.finish()
-    tp_ring.finish()
+    tp_ring.arrive(0, 5)
     local[0].wait()
 
-    totals[...] = jnp.zeros_like(totals)
-    squares[...] = jnp.zeros_like(squares)
-
-    def project(b, _):
+    def project(j, _):
+        b = arrival(j)
         wide = blocks[b].astype(jnp.float32)
         part = wide * wide
         squares[...] += sum(part[:, k * HD : (k + 1) * HD] for k in range(part.shape[1] // HD))
@@ -442,14 +505,20 @@
         totals[...] += jnp.dot(low, weights[b], preferred_element_type=jnp.float32)
         return 0
 
-    lax.fori_loop(0, 8, project, 0)
+    lax.fori_loop(0, 10, project, 0)
+    tp_ring.step(4)
+    sums.first()
     sums.first_high()
-    out_ring.send_side()
-    lax.fori_loop(8, 16, project, 0)
+    turn.rise()
+    old_ring.near("own")
+    tp_ring.arrive(5, 9)
+    sums.cross(3, -3)
+    lax.fori_loop(10, 16, project, 0)
     width = 16 * stream.shape[1]
     mean_square = jnp.sum(squares[...], axis=1, keepdims=True) / width
     scale = lax.rsqrt(mean_square + NORM_EPSILON)
-    cos, sin = cosine[...], sinus[...]
+    cos = jnp.concatenate([cosine[...], cosine[...]], axis=1)
+    sin = jnp.concatenate([-sinus[...], sinus[...]], axis=1)
 
     def rotate(part):
         return part * cos + pltpu.roll(part, HD // 2, 1) * sin
@@ -469,7 +538,7 @@
     sent = [net.push(made, "xl", fresh.at[xl, 2])]
     for (ahead, _), device in later.items():
         sent.append(net.push(made, device, fresh.at[xl, 2 - ahead]))
-    sums.step(1)
+    sums.step(1, (0, 1))
 
     to_exponent = math.log2(math.e) / math.sqrt(HD)
     for h in range(heads):
@@ -479,7 +548,7 @@
     top[...] = jnp.full_like(top, MASKED)
     total[...] = jnp.zeros_like(total)
     mix[...] = jnp.zeros_like(mix)
-    own_marks = q_marks[...]
+    own_marks = q_marks[:, :1]
 
     def absorb(h, keys, values, seen):
         scores = lax.dot_general(
@@ -496,10 +565,6 @@
         )
         top[h] = now
 
-    def row_of(marks, first, count):
-        wide = marks.astype(jnp.float32)
-        return jnp.concatenate([wide[first + k : first + k + 1] for k in range(count)], axis=1)
-
     def over_prefix(i, _):
         def on(k, *actions):
             @pl.when(i == k)
@@ -510,9 +575,10 @@
         for k in range(16):
             if k in before_block:
                 on(k, *before_block[k])
-        group = i // 4
-        turn_y = jnp.where(group == 1, 3, jnp.where(group == 2, 1, jnp.where(group == 3, 2, 0)))
-        at = ctx_of((y + turn_y) % 4, (xh + (i // 2) % 2) % 2, (core + i % 2) % 2)
+        group, beside = i // 4, (i // 2) % 2
+        turn_y = jnp.where(group == 0, 0, jnp.where(group == 3, 2, 3 - 2 * beside))
+        turn_x = jnp.where(group == 1, 0, jnp.where(group == 2, 1, beside))
+        at = ctx_of((y + turn_y) % 4, (xh + turn_x) % 2, (core + i % 2) % 2)
         marks = row_of(cache[at, 2 * span :], 0, span // HD)
         seen = marks <= own_marks
         for h in range(heads):
@@ -526,19 +592,31 @@
 
         return wait
 
+    def start_out():
+        turn.finish()
+        out_ring.send_own()
+        out_ring.send_across()
+
     before_block = {
         0: [sib(old_ring, 0, 1)],
-        2: [lambda: old_ring.step(2), lambda: out_ring.step(1)],
-        4: [sib(old_ring, 2, 3)],
-        6: [lambda: sums.step(2)],
-        8: [sib(old_ring, 4, 5), lambda: out_ring.step(2)],
-        12: [sib(old_ring, 6, 7)],
-        13: [lambda: sums.step(3)],
+        2: [lambda: sums.cross(2, -2)],
+        3: [lambda: sums.step(1, (2,)), lambda: old_ring.near("side")],
+        4: [sib(old_ring, 2, 3), turn.finish, out_ring.send_across],
+        5: [lambda: sums.cross(1, -1, 0)],
+        6: [lambda: sums.step(2, (0, 1)), old_ring.far],
+        7: [out_ring.send_own],
+        8: [sib(old_ring, 4, 5)],
+        9: [lambda: sums.step(2, (2,))],
+        11: [out_ring.send_side],
+        12: [sib(old_ring, 6, 7), lambda: sums.step(3, (0, 1))],
+        13: [lambda: out_ring.near("own")],
+        15: [lambda: sums.step(3, (2,))],
     }
     lax.fori_loop(0, 16, over_prefix, 0)
     for copy in sent:
         copy.wait_recv()
     keep.wait()
+    out_ring.near("side")
     for j in range(3):
         back = 2 - j
         row = row_of(cache[(c + 16 - back) % 16, 2 * span :], span // HD, rows // HD)
@@ -553,32 +631,44 @@
     for h in range(heads):
         attended[:, h * HD : (h + 1) * HD] = (mix[h] / total[h]).astype(jnp.bfloat16)
 
-    ring = TpRing(net, attended, gathered)
+    ring = TpRing(net, attended, gathered, 208)
     gathered[t] = attended[...]
+    ring.cross()
     sums.last_other()
+    out_ring.far()
+    ring.step(1)
     out_ring.finish()
-    own_out.wait()
-    ring.cross()
-    for step in (1, 2, 3, 4):
-        ring.step(step)
     low, high = sums.last()
     half = rows // 2
-    total_out[:half] = low
-    total_out[half:] = high
-    ring.finish()
-
-    def project_out(b, _):
-        total_out[...] += jnp.dot(gathered[b], out_rows[b], preferred_element_type=jnp.float32)
+    total_out[:half] = low + blocks[t, :half].astype(jnp.float32)
+    total_out[half:] = high + blocks[t, half:].astype(jnp.float32)
+
+    def project_out(j, _):
+        b = arrival(j)
+        part = out_rows[b // 2, b % 2].reshape(q_cols, stream.shape[1])
+        total_out[...] += jnp.dot(gathered[b], part, preferred_element_type=jnp.float32)
         return 0
 
-    lax.fori_loop(0, 16, project_out, 0)
-    output[...] = (blocks[t].astype(jnp.float32) + total_out[...]).astype(jnp.bfloat16)
+    ring.arrive(0, 1)
+    lax.fori_loop(0, 2, project_out, 0)
+    ring.step(2)
+    ring.arrive(1, 3)
+    lax.fori_loop(2, 6, project_out, 0)
+    ring.step(3)
+    ring.arrive(3, 5)
+    lax.fori_loop(6, 10, project_out, 0)
+    ring.step(4)
+    ring.arrive(5, 7)
+    lax.fori_loop(10, 14, project_out, 0)
+    ring.arrive(7, 9)
+    lax.fori_loop(14, 16, project_out, 0)
+    output[...] = total_out[...].astype(jnp.bfloat16)
     net.drain()
     assert len(net.copies) <= COPIES
 
 
 def run_block(stream, pending, w_query, w_key, w_value, w_out, old_keys, old_values, labels,
-              gain, cosine, sinus, q_marks):
+              gain, cosine, sinus):
     rows, cols = stream.shape
     depth, q_cols = w_query.shape
     span = old_keys.shape[1]
@@ -590,13 +680,13 @@
     return pl.pallas_call(
         block_kernel,
         out_shape=jax.ShapeDtypeStruct((rows, cols), low),
-        in_specs=[any_spec] * 9 + [vmem] * 4,
+        in_specs=[any_spec] * 9 + [vmem] * 3,
         out_specs=vmem,
         scratch_shapes=[
             pltpu.VMEM((16, rows, cols), low),
             pltpu.VMEM((16, depth, q_cols + HD), low),
             pltpu.VMEM((16, 2 * span + LABEL_ROWS, HD), low),
-            pltpu.VMEM((16, *w_out.shape), low),
+            pltpu.VMEM((8, 2, 8, w_out.shape[0] // 8, w_out.shape[1]), low),
             pltpu.VMEM((16, rows, q_cols), low),
             pltpu.VMEM((16, rows, cols), low),
             pltpu.VMEM((8, half, cols), low),
@@ -608,9 +698,10 @@
             pltpu.VMEM((heads, rows, HD), low),
             pltpu.VMEM((rows, HD), low),
             pltpu.VMEM((2, 3, rows, HD), low),
-            pltpu.VMEM(w_out.shape, low),
+            pltpu.VMEM((8, w_out.shape[0] // 8, w_out.shape[1]), low),
             pltpu.VMEM((rows, q_cols), low),
             pltpu.VMEM((rows, cols), wide),
+            pltpu.VMEM((rows, HD), wide),
             pltpu.VMEM((heads, rows, HD), wide),
             pltpu.VMEM((heads, rows, HD), wide),
             pltpu.VMEM((heads, rows, HD), wide),
@@ -618,14 +709,14 @@
             pltpu.SemaphoreType.DMA((16,)),
             pltpu.SemaphoreType.DMA((COPIES,)),
             pltpu.SemaphoreType.DMA((COPIES,)),
-            pltpu.SemaphoreType.DMA((3,)),
+            pltpu.SemaphoreType.DMA((4,)),
         ],
         compiler_params=pltpu.CompilerParams(
             collective_id=0, has_side_effects=True, vmem_limit_bytes=58 << 20
         ),
         name="attention_block",
     )(stream, pending, w_query, w_key, w_value, w_out, old_keys, old_values, labels,
-      gain, cosine, sinus, q_marks)
+      gain, cosine, sinus)
 
 
 def per_device(
@@ -646,16 +737,13 @@
     token = lax.axis_index("ctx") * rows + jnp.arange(rows, dtype=jnp.int32)
     positions = stretch_offset[0].astype(jnp.float32) + token.astype(jnp.float32)
     angles = positions[:, None] * inverse_freqs(HD)
-    cos, sin = jnp.cos(angles), jnp.sin(angles)
-    cosine = jnp.concatenate([cos, cos], axis=1)
-    sinus = jnp.concatenate([-sin, sin], axis=1)
+    cosine, sinus = jnp.cos(angles), jnp.sin(angles)
     labels = jnp.concatenate([prefix_segments, stretch_segments]).reshape(-1, HD)
     labels = jnp.pad(labels, ((0, LABEL_ROWS - labels.shape[0]), (0, 0))).astype(jnp.bfloat16)
     gain = norm_gain.astype(jnp.float32).reshape(16, 1, cols)
-    q_marks = stretch_segments.astype(jnp.float32)[:, None]
     return run_block(
         stream, pending, w_query, w_key, w_value, w_out, prefix_keys, prefix_values, labels,
-        gain, cosine, sinus, q_marks,
+        gain, cosine, sinus,
     )
 
 

time: 192 us -> 152 us (0.79)
  Pallas kernels: 185 us -> 143 us
    pallas_call x1, Pallas kernels: 185 us -> 143 us  [run_block(): pl.pallas_call(block_kernel, out_shape=jax.ShapeDtypeStruct((rows, cols),...]
where the time goes in v3:
time: 152 us; the launch traced here: 150 us
  Pallas kernels  143 us (94%)
  other arithmetic  4.26 us (3%)
  local copies, waits for them, and re-layouts  2.37 us (2%)
    pallas_call x1, Pallas kernels, run_block(): pl.pallas_call(block_kernel, out_shape=jax.ShapeDtypeStruct((rows, cols),...  143 us

profile of v3, /device:TPU:4, one launch (start us, length us, event | category | flops | bytes accessed | tf_op | source)
XLA Modules:
  0.0 150.0 jit_solution(9900532707664851085)
XLA Ops:
  0.7 0.7 convert.11
  1.4 0.7 convert.10
  2.1 0.6 pad.5.labels
  2.7 1.3 reshape.40
  4.0 1.5 %multiply_sine_fusion = (f32[384,64]{1,0:T(8,128)}, f32[384,64]{1,0:T(8,128)}) fusion(f32[64]{0:T(128)S(1)} %compare_select_fusion.1, f32[384]{0:T(512)S(1)} %convert_add_fusion), kind=kLoop, calls=%fused_computation | loop fusion | flops 24576 | bytes 198400 | tf_op jit(solution)/shard_map/sin | solution.py:740
  5.5 142.7 %attention_block.1 = bf16[384,512]{1,0:T(8,128)(2,1)} custom-call(bf16[384,512]{1,0:T(8,128)(2,1)} %stream.1, bf16[1,384,8192]{2,1,0:T(8,128)(2,1)} %pending.1, bf16[512,256]{1,0:T(8,128)(2,1)} %w_query.1, bf16[512,1024]{1,0:T(8,128)(2,1)} %w_key.1, bf16[512,1024]{1,0:T(8,128)(2,1)} %w_value.1, bf16[256,512]{1,0:T(8,128)(2,1)} %w_out.1, ...), custom_call_target="tpu_custom_call" | custom-call | tf_op jit(solution)/shard_map/attention_block/pallas_call | solution.py:680
  148.2 1.8 %copy.15 = bf16[384,512]{1,0:T(8,128)(2,1)} copy(bf16[384,512]{1,0:T(8,128)(2,1)} %attention_block.1) | data formatting | bytes 786432
  (3 shorter events, 0.0 us)

commit v4 on v3

--- a/solution.py
+++ b/solution.py
@@ -3,6 +3,7 @@
 
 import jax
 import jax.numpy as jnp
+import numpy as np
 from jax import lax
 from jax.experimental import pallas as pl
 from jax.experimental.pallas import tpu as pltpu
@@ -21,16 +22,17 @@
 
 
 def inverse_freqs(head_width):
-    pair_index = jnp.arange(head_width // 2, dtype=jnp.float32)
+    pair_index = np.arange(head_width // 2, dtype=np.float64)
     base_freq = ROPE_BASE ** (-2.0 * pair_index / head_width)
     wavelength = 2.0 * math.pi / base_freq
     smooth = (INITIAL_SPAN / wavelength - LOW_FREQ) / (HIGH_FREQ - LOW_FREQ)
     blended = (1.0 - smooth) * base_freq / ROPE_FACTOR + smooth * base_freq
-    return jnp.where(
+    chosen = np.where(
         wavelength < INITIAL_SPAN / HIGH_FREQ,
         base_freq,
-        jnp.where(wavelength > INITIAL_SPAN / LOW_FREQ, base_freq / ROPE_FACTOR, blended),
+        np.where(wavelength > INITIAL_SPAN / LOW_FREQ, base_freq / ROPE_FACTOR, blended),
     )
+    return chosen.astype(np.float32)
 
 
 def coords():
@@ -71,9 +73,9 @@
 
 
 class Copy:
-    def __init__(self, net, k, ref, device):
+    def __init__(self, net, k, sent, ref, device):
         self.root, self.shape = getattr(ref, "ref", ref), ref.shape
-        self.net, self.k, self.device = net, k, device
+        self.net, self.k, self.sent, self.device = net, k, sent, device
 
     def handle(self):
         lead = (0,) * (len(self.root.shape) - len(self.shape))
@@ -81,7 +83,7 @@
         return pltpu.make_async_remote_copy(
             src_ref=like,
             dst_ref=like,
-            send_sem=self.net.send_sem.at[self.k],
+            send_sem=self.net.send_sem.at[self.sent],
             recv_sem=self.net.recv_sem.at[self.k],
             device_id=self.device,
             device_id_type=MESH,
@@ -97,25 +99,32 @@
 class Net:
     def __init__(self, links, send_sem, recv_sem):
         self.links, self.send_sem, self.recv_sem = links, send_sem, recv_sem
-        self.copies = []
+        self.count, self.under_way, self.spare, self.used = 0, [], [], 0
 
     def push(self, src, link, dst=None):
-        k = len(self.copies)
+        k, self.count = self.count, self.count + 1
+        if self.spare:
+            sent = self.spare.pop(0)
+        else:
+            sent, self.used = self.used, self.used + 1
         device = self.links[link] if isinstance(link, str) else link
         pltpu.make_async_remote_copy(
             src_ref=src,
             dst_ref=src if dst is None else dst,
-            send_sem=self.send_sem.at[k],
+            send_sem=self.send_sem.at[sent],
             recv_sem=self.recv_sem.at[k],
             device_id=device,
             device_id_type=MESH,
         ).start()
-        self.copies.append(Copy(self, k, src, device))
-        return self.copies[-1]
-
-    def drain(self):
-        for copy in self.copies:
+        self.under_way.append(Copy(self, k, sent, src, device))
+        return self.under_way[-1]
+
+    def drain(self, before=None):
+        done = [copy for copy in self.under_way if before is None or copy.k < before]
+        self.under_way = [copy for copy in self.under_way if copy not in done]
+        for copy in done:
             copy.wait_send()
+        self.spare += [copy.sent for copy in done]
 
 
 class TpRing:
@@ -285,14 +294,18 @@
 
 
 class PendingSum:
-    def __init__(self, net, pending, slabs, crossed, landed, landed_parts, final, sems):
+    def __init__(
+        self, net, pending, slabs, crossed, landed, landed_high, landed_parts, final, sems
+    ):
         self.net, self.slabs, self.crossed = net, slabs, crossed
-        self.landed, self.landed_parts, self.final = landed, landed_parts, final
+        self.landed, self.landed_high = landed, landed_high
+        self.landed_parts, self.final = landed_parts, final
         _, _, _, self.z, self.xl = coords()
         rows, cols = slabs.shape[1:]
-        half, quarter = rows // 2, rows // 4
-        self.low, self.high = pl.ds(0, half), pl.ds(half, half)
-        self.parts = (pl.ds(half, quarter), pl.ds(half + quarter, quarter))
+        upper, part = crossed.shape[1], landed_parts.shape[1]
+        self.half = rows - upper
+        self.low, self.high = pl.ds(0, self.half), pl.ds(self.half, upper)
+        self.parts = (pl.ds(self.half, part), pl.ds(self.half + part, upper - part))
         self.loads = [
             pltpu.make_async_copy(
                 pending.at[0, :, pl.ds(k * cols, cols)], slabs.at[k], sems.at[k]
@@ -329,6 +342,8 @@
     def land(self, way, kind, step):
         if kind == 2 and step == 0:
             return self.landed_parts.at[way]
+        if kind == 2:
+            return self.landed_high.at[way, step - 1]
         return self.landed.at[way, kind, step]
 
     def send(self, way, kind, step, index, rows):
@@ -376,22 +391,24 @@
         low = self.slabs[self.at(0), self.low].astype(wide) + self.final[...].astype(wide)
         low = low + self.landed[0, 0, 3].astype(wide) + self.landed[1, 0, 3].astype(wide)
         high = self.slabs[self.at(0), self.high].astype(wide) + self.crossed[self.z].astype(wide)
-        high = high + self.landed[0, 2, 3].astype(wide) + self.landed[1, 2, 3].astype(wide)
+        high = high + self.landed_high[0, 2].astype(wide) + self.landed_high[1, 2].astype(wide)
         return low, high
 
 
-COPIES = 256
+COPIES = 159
+UPPER = 192
+SENDS = 87
 
 
 def block_kernel(
-    stream, pending, w_query, w_key, w_value, w_out, old_keys, old_values, labels,
-    gain, cosine, sinus,
+    stream, pending, w_query, w_key, w_value, w_out, old_keys, old_values,
+    prefix_labels, stretch_labels, gain, freqs, offset,
     output,
     blocks, weights, cache, out_rows, gathered,
-    slabs, crossed, landed, landed_parts, final,
-    totals, squares, query, made, fresh, mid, attended, total_out, q_marks,
+    slabs, crossed, landed, landed_high, landed_parts, final,
+    totals, squares, query, made, fresh, mid, attended, total_out, q_marks, labels, cosine, sinus, gains,
     top, total, mix,
-    local_sem, load_sem, send_sem, recv_sem, turn_sem,
+    local_sem, label_sem, load_sem, send_sem, recv_sem, turn_sem,
 ):
     y, xh, core, z, xl = coords()
     c, t = ctx_of(y, xh, core), tp_of(z, xl)
@@ -414,13 +431,18 @@
         pltpu.make_async_copy(w_query, weights.at[c, :, pl.ds(0, q_cols)], local_sem.at[1]),
         pltpu.make_async_copy(old_keys.at[z], cache.at[c, pl.ds(0, span)], local_sem.at[2]),
         pltpu.make_async_copy(old_values.at[z], cache.at[c, pl.ds(span, span)], local_sem.at[3]),
-        pltpu.make_async_copy(labels, cache.at[c, pl.ds(2 * span, LABEL_ROWS)], local_sem.at[4]),
+    ]
+    marks_here = [
+        pltpu.make_async_copy(ref.at[pl.ds(k * HD, HD)], labels.at[row], label_sem.at[row])
+        for ref, k, row in [(prefix_labels, k, k) for k in range(span // HD)]
+        + [(stretch_labels, k, span // HD + k) for k in range(rows // HD)]
     ]
     head_cols = pl.ds(pl.multiple_of(z * HD, HD), HD)
     kv_slot = weights.at[c, :, pl.ds(q_cols, HD)]
     key_copy = pltpu.make_async_copy(w_key.at[:, head_cols], kv_slot, local_sem.at[5])
     value_copy = pltpu.make_async_copy(w_value.at[:, head_cols], kv_slot, local_sem.at[5])
-    for copy in local:
+    labels[...] = jnp.zeros_like(labels)
+    for copy in local + marks_here:
         copy.start()
 
     @pl.when(xl == 0)
@@ -463,19 +485,31 @@
     w_ring = CtxRing(net, weights.at[c], lambda k: weights.at[k], "xh")
     w_ring.send_own()
     w_ring.send_across()
-    for k in (2, 3, 4):
-        local[k].wait()
+    for copy in local[2:] + marks_here:
+        copy.wait()
+    cache[c, 2 * span :] = labels[...].astype(jnp.float32).astype(jnp.bfloat16)
     old_ring = CtxRing(net, cache.at[c], lambda k: cache.at[k], "xd")
     out_ring = CtxRing(
         net, turn.own(pl.ds(0, 8)), lambda k: out_rows.at[:, k % 2, k // 2], "xh"
     )
-    sums = PendingSum(net, pending, slabs, crossed, landed, landed_parts, final, load_sem)
+    sums = PendingSum(net, pending, slabs, crossed, landed, landed_high, landed_parts, final, load_sem)
     row = row_of(cache[c, 2 * span :], span // HD, rows // HD)
     flat = (rows, rows)
     diagonal = lax.broadcasted_iota(jnp.int32, flat, 0) == lax.broadcasted_iota(jnp.int32, flat, 1)
     q_marks[...] = jnp.sum(jnp.where(diagonal, row, 0.0), axis=1, keepdims=True) + jnp.zeros(
         (rows, HD), jnp.float32
     )
+    token = (c * rows + lax.broadcasted_iota(jnp.int32, (rows, HD), 0)).astype(jnp.float32)
+    angles = (offset[0].astype(jnp.float32) + token) * freqs[...]
+    turns = jnp.floor(angles * (0.5 / math.pi) + 0.5)
+    angles = (angles - turns * 6.28125) - turns * (2.0 * math.pi - 6.28125)
+    cosine[...] = jnp.cos(angles)
+    lower = lax.broadcasted_iota(jnp.int32, (rows, HD), 1) < HD // 2
+    sinus[...] = jnp.where(lower, -1.0, 1.0) * jnp.sin(angles)
+    wide_gain = gain[...].astype(jnp.float32)
+    per_block = stream.shape[1] // HD
+    for b in range(16):
+        gains[b] = row_of(wide_gain, b * per_block, per_block)
     totals[...] = jnp.zeros_like(totals)
     squares[...] = jnp.zeros_like(squares)
     tp_ring.cross()
@@ -487,6 +521,7 @@
     tp_ring.step(2)
     w_ring.near("side")
     w_ring.far()
+    early = net.count
     old_ring.send_own()
     old_ring.send_side()
     tp_ring.step(3)
@@ -501,7 +536,7 @@
         wide = blocks[b].astype(jnp.float32)
         part = wide * wide
         squares[...] += sum(part[:, k * HD : (k + 1) * HD] for k in range(part.shape[1] // HD))
-        low = (wide * gain[b]).astype(jnp.bfloat16)
+        low = (wide * gains[b]).astype(jnp.bfloat16)
         totals[...] += jnp.dot(low, weights[b], preferred_element_type=jnp.float32)
         return 0
 
@@ -517,11 +552,8 @@
     width = 16 * stream.shape[1]
     mean_square = jnp.sum(squares[...], axis=1, keepdims=True) / width
     scale = lax.rsqrt(mean_square + NORM_EPSILON)
-    cos = jnp.concatenate([cosine[...], cosine[...]], axis=1)
-    sin = jnp.concatenate([-sinus[...], sinus[...]], axis=1)
-
     def rotate(part):
-        return part * cos + pltpu.roll(part, HD // 2, 1) * sin
+        return part * cosine[...] + pltpu.roll(part, HD // 2, 1) * sinus[...]
 
     part = totals[:, 2 * HD :] * scale
 
@@ -545,6 +577,8 @@
         part = totals[:, h * HD : (h + 1) * HD] * scale
         query[h] = (rotate(part) * to_exponent).astype(jnp.bfloat16)
 
+    net.drain(early)
+    early = net.count
     top[...] = jnp.full_like(top, MASKED)
     total[...] = jnp.zeros_like(total)
     mix[...] = jnp.zeros_like(mix)
@@ -599,17 +633,17 @@
 
     before_block = {
         0: [sib(old_ring, 0, 1)],
-        2: [lambda: sums.cross(2, -2)],
-        3: [lambda: sums.step(1, (2,)), lambda: old_ring.near("side")],
-        4: [sib(old_ring, 2, 3), turn.finish, out_ring.send_across],
-        5: [lambda: sums.cross(1, -1, 0)],
+        1: [lambda: sums.cross(2, -2)],
+        4: [lambda: sums.step(1, (2,)), lambda: old_ring.near("side"), sib(old_ring, 2, 3)],
+        5: [turn.finish, out_ring.send_across],
         6: [lambda: sums.step(2, (0, 1)), old_ring.far],
         7: [out_ring.send_own],
         8: [sib(old_ring, 4, 5)],
-        9: [lambda: sums.step(2, (2,))],
-        11: [out_ring.send_side],
-        12: [sib(old_ring, 6, 7), lambda: sums.step(3, (0, 1))],
-        13: [lambda: out_ring.near("own")],
+        9: [lambda: sums.step(2, (2,)), lambda: sums.cross(1, -1, 0)],
+        11: [lambda: sums.step(3, (0, 1))],
+        12: [sib(old_ring, 6, 7)],
+        13: [out_ring.send_side],
+        14: [lambda: out_ring.near("own")],
         15: [lambda: sums.step(3, (2,))],
     }
     lax.fori_loop(0, 16, over_prefix, 0)
@@ -631,6 +665,7 @@
     for h in range(heads):
         attended[:, h * HD : (h + 1) * HD] = (mix[h] / total[h]).astype(jnp.bfloat16)
 
+    net.drain(early)
     ring = TpRing(net, attended, gathered, 208)
     gathered[t] = attended[...]
     ring.cross()
@@ -639,9 +674,8 @@
     ring.step(1)
     out_ring.finish()
     low, high = sums.last()
-    half = rows // 2
-    total_out[:half] = low + blocks[t, :half].astype(jnp.float32)
-    total_out[half:] = high + blocks[t, half:].astype(jnp.float32)
+    total_out[: sums.half] = low + blocks[t, : sums.half].astype(jnp.float32)
+    total_out[sums.half :] = high + blocks[t, sums.half :].astype(jnp.float32)
 
     def project_out(j, _):
         b = arrival(j)
@@ -664,23 +698,22 @@
     lax.fori_loop(14, 16, project_out, 0)
     output[...] = total_out[...].astype(jnp.bfloat16)
     net.drain()
-    assert len(net.copies) <= COPIES
-
-
-def run_block(stream, pending, w_query, w_key, w_value, w_out, old_keys, old_values, labels,
-              gain, cosine, sinus):
+    assert net.count == COPIES and net.used == SENDS, (net.count, net.used)
+
+
+def run_block(stream, pending, w_query, w_key, w_value, w_out, old_keys, old_values,
+              prefix_labels, stretch_labels, gain, freqs, offset):
     rows, cols = stream.shape
     depth, q_cols = w_query.shape
     span = old_keys.shape[1]
     low, wide = jnp.bfloat16, jnp.float32
-    half = rows // 2
     any_spec = pl.BlockSpec(memory_space=pl.ANY)
     vmem = pl.BlockSpec(memory_space=pltpu.VMEM)
     heads = q_cols // HD
     return pl.pallas_call(
         block_kernel,
         out_shape=jax.ShapeDtypeStruct((rows, cols), low),
-        in_specs=[any_spec] * 9 + [vmem] * 3,
+        in_specs=[any_spec] * 10 + [vmem] * 2 + [pl.BlockSpec(memory_space=pltpu.SMEM)],
         out_specs=vmem,
         scratch_shapes=[
             pltpu.VMEM((16, rows, cols), low),
@@ -689,10 +722,11 @@
             pltpu.VMEM((8, 2, 8, w_out.shape[0] // 8, w_out.shape[1]), low),
             pltpu.VMEM((16, rows, q_cols), low),
             pltpu.VMEM((16, rows, cols), low),
-            pltpu.VMEM((8, half, cols), low),
-            pltpu.VMEM((2, 3, 4, half, cols), low),
-            pltpu.VMEM((2, half // 2, cols), low),
-            pltpu.VMEM((half, cols), low),
+            pltpu.VMEM((8, UPPER, cols), low),
+            pltpu.VMEM((2, 2, 4, rows - UPPER, cols), low),
+            pltpu.VMEM((2, 3, UPPER, cols), low),
+            pltpu.VMEM((2, UPPER // 2, cols), low),
+            pltpu.VMEM((rows - UPPER, cols), low),
             pltpu.VMEM((rows, q_cols + HD), wide),
             pltpu.VMEM((rows, HD), wide),
             pltpu.VMEM((heads, rows, HD), low),
@@ -702,12 +736,17 @@
             pltpu.VMEM((rows, q_cols), low),
             pltpu.VMEM((rows, cols), wide),
             pltpu.VMEM((rows, HD), wide),
+            pltpu.VMEM((LABEL_ROWS, HD), jnp.int32),
+            pltpu.VMEM((rows, HD), wide),
+            pltpu.VMEM((rows, HD), wide),
+            pltpu.VMEM((16, 1, cols), wide),
             pltpu.VMEM((heads, rows, HD), wide),
             pltpu.VMEM((heads, rows, HD), wide),
             pltpu.VMEM((heads, rows, HD), wide),
             pltpu.SemaphoreType.DMA((8,)),
+            pltpu.SemaphoreType.DMA((LABEL_ROWS,)),
             pltpu.SemaphoreType.DMA((16,)),
-            pltpu.SemaphoreType.DMA((COPIES,)),
+            pltpu.SemaphoreType.DMA((SENDS,)),
             pltpu.SemaphoreType.DMA((COPIES,)),
             pltpu.SemaphoreType.DMA((4,)),
         ],
@@ -715,8 +754,8 @@
             collective_id=0, has_side_effects=True, vmem_limit_bytes=58 << 20
         ),
         name="attention_block",
-    )(stream, pending, w_query, w_key, w_value, w_out, old_keys, old_values, labels,
-      gain, cosine, sinus)
+    )(stream, pending, w_query, w_key, w_value, w_out, old_keys, old_values,
+      prefix_labels, stretch_labels, gain, freqs, offset)
 
 
 def per_device(
@@ -733,17 +772,11 @@
     stretch_segments,
     stretch_offset,
 ):
-    rows, cols = stream.shape
-    token = lax.axis_index("ctx") * rows + jnp.arange(rows, dtype=jnp.int32)
-    positions = stretch_offset[0].astype(jnp.float32) + token.astype(jnp.float32)
-    angles = positions[:, None] * inverse_freqs(HD)
-    cosine, sinus = jnp.cos(angles), jnp.sin(angles)
-    labels = jnp.concatenate([prefix_segments, stretch_segments]).reshape(-1, HD)
-    labels = jnp.pad(labels, ((0, LABEL_ROWS - labels.shape[0]), (0, 0))).astype(jnp.bfloat16)
-    gain = norm_gain.astype(jnp.float32).reshape(16, 1, cols)
+    freqs = inverse_freqs(HD)
     return run_block(
-        stream, pending, w_query, w_key, w_value, w_out, prefix_keys, prefix_values, labels,
-        gain, cosine, sinus,
+        stream, pending, w_query, w_key, w_value, w_out, prefix_keys, prefix_values,
+        prefix_segments, stretch_segments, norm_gain.reshape(-1, HD),
+        jnp.asarray(np.concatenate([freqs, freqs])[None]), stretch_offset,
     )
 
 

time: 152 us -> 144 us (0.947); the launches traced: 150 us -> 144 us
  other arithmetic: 4.26 us -> 0 us
where the time goes in v4:
time: 144 us
  Pallas kernels  142 us (99%)
  local copies, waits for them, and re-layouts  1.77 us (1%)
    pallas_call x1, Pallas kernels, run_block(): pl.pallas_call(block_kernel, out_shape=jax.ShapeDtypeStruct((rows, cols),...  142 us

profile of v4, /device:TPU:4, one launch (start us, length us, event | category | flops | bytes accessed | tf_op | source)
XLA Modules:
  0.0 144.0 jit_solution(2644795552489110773)
XLA Ops:
  0.7 141.6 %attention_block.1 = bf16[384,512]{1,0:T(8,128)(2,1)} custom-call(bf16[384,512]{1,0:T(8,128)(2,1)} %stream.1, bf16[1,384,8192]{2,1,0:T(8,128)(2,1)} %pending.1, bf16[512,256]{1,0:T(8,128)(2,1)} %w_query.1, bf16[512,1024]{1,0:T(8,128)(2,1)} %w_key.1, bf16[512,1024]{1,0:T(8,128)(2,1)} %w_value.1, bf16[256,512]{1,0:T(8,128)(2,1)} %w_out.1, ...), custom_call_target="tpu_custom_call" | custom-call | tf_op jit(solution)/shard_map/attention_block/pallas_call | solution.py:713
  142.3 1.8 %copy.16 = bf16[384,512]{1,0:T(8,128)(2,1)} copy(bf16[384,512]{1,0:T(8,128)(2,1)} %attention_block.1) | data formatting | bytes 786432

commit v5 on v4

--- a/solution.py
+++ b/solution.py
@@ -308,20 +308,19 @@
         self.parts = (pl.ds(self.half, part), pl.ds(self.half + part, upper - part))
         self.loads = [
             pltpu.make_async_copy(
-                pending.at[0, :, pl.ds(k * cols, cols)], slabs.at[k], sems.at[k]
+                pending.at[0, :, pl.ds(k * cols, cols)], slabs.at[k], sems.at[0]
             )
             for k in range(16)
         ]
         for load in self.loads:
             load.start()
-        self.hop, self.over = {}, {}
+        self.hop, self.over, self.sems = {}, {}, sems
 
     def at(self, offset, other=0):
         return tp_of((self.z + offset + 8) % 8, (self.xl + other) % 2)
 
     def ready(self):
-        for load in self.loads:
-            load.wait()
+        pltpu.make_async_copy(self.slabs, self.slabs, self.sems.at[0]).wait()
 
     def cross(self, *offsets):
         for offset in offsets:
@@ -397,7 +396,7 @@
 
 COPIES = 159
 UPPER = 192
-SENDS = 87
+SENDS = 56
 
 
 def block_kernel(
@@ -513,14 +512,18 @@
     totals[...] = jnp.zeros_like(totals)
     squares[...] = jnp.zeros_like(squares)
     tp_ring.cross()
+    starts = net.count
     turn.spread()
     w_ring.near("own")
     tp_ring.step(1)
     w_ring.send_side()
     old_ring.send_across()
+    first = net.count
     tp_ring.step(2)
+    net.drain(starts)
     w_ring.near("side")
     w_ring.far()
+    net.drain(first)
     early = net.count
     old_ring.send_own()
     old_ring.send_side()
@@ -542,6 +545,7 @@
 
     lax.fori_loop(0, 10, project, 0)
     tp_ring.step(4)
+    net.drain(early)
     sums.first()
     sums.first_high()
     turn.rise()
@@ -578,7 +582,7 @@
         query[h] = (rotate(part) * to_exponent).astype(jnp.bfloat16)
 
     net.drain(early)
-    early = net.count
+    sent_before = net.count
     top[...] = jnp.full_like(top, MASKED)
     total[...] = jnp.zeros_like(total)
     mix[...] = jnp.zeros_like(mix)
@@ -639,7 +643,7 @@
         6: [lambda: sums.step(2, (0, 1)), old_ring.far],
         7: [out_ring.send_own],
         8: [sib(old_ring, 4, 5)],
-        9: [lambda: sums.step(2, (2,)), lambda: sums.cross(1, -1, 0)],
+        9: [lambda: net.drain(sent_before), lambda: sums.step(2, (2,)), lambda: sums.cross(1, -1, 0)],
         11: [lambda: sums.step(3, (0, 1))],
         12: [sib(old_ring, 6, 7)],
         13: [out_ring.send_side],
@@ -665,7 +669,7 @@
     for h in range(heads):
         attended[:, h * HD : (h + 1) * HD] = (mix[h] / total[h]).astype(jnp.bfloat16)
 
-    net.drain(early)
+    net.drain(net.count - 16)
     ring = TpRing(net, attended, gathered, 208)
     gathered[t] = attended[...]
     ring.cross()
@@ -744,8 +748,8 @@
             pltpu.VMEM((heads, rows, HD), wide),
             pltpu.VMEM((heads, rows, HD), wide),
             pltpu.SemaphoreType.DMA((8,)),
-            pltpu.SemaphoreType.DMA((LABEL_ROWS,)),
-            pltpu.SemaphoreType.DMA((16,)),
+            pltpu.SemaphoreType.DMA(((span + rows) // HD,)),
+            pltpu.SemaphoreType.DMA((1,)),
             pltpu.SemaphoreType.DMA((SENDS,)),
             pltpu.SemaphoreType.DMA((COPIES,)),
             pltpu.SemaphoreType.DMA((4,)),

time: 144 us -> 144 us (level)
  no operation moved by 1% of the time
where the time goes in v5:
time: 144 us
  Pallas kernels  141 us (98%)
  local copies, waits for them, and re-layouts  1.77 us (1%)
    pallas_call x1, Pallas kernels, run_block(): pl.pallas_call(block_kernel, out_shape=jax.ShapeDtypeStruct((rows, cols),...  141 us

profile of v5, /device:TPU:4, one launch (start us, length us, event | category | flops | bytes accessed | tf_op | source)
XLA Modules:
  0.0 143.6 jit_solution(13103460594302946069)
XLA Ops:
  0.7 141.1 %attention_block.1 = bf16[384,512]{1,0:T(8,128)(2,1)} custom-call(bf16[384,512]{1,0:T(8,128)(2,1)} %stream.1, bf16[1,384,8192]{2,1,0:T(8,128)(2,1)} %pending.1, bf16[512,256]{1,0:T(8,128)(2,1)} %w_query.1, bf16[512,1024]{1,0:T(8,128)(2,1)} %w_key.1, bf16[512,1024]{1,0:T(8,128)(2,1)} %w_value.1, bf16[256,512]{1,0:T(8,128)(2,1)} %w_out.1, ...), custom_call_target="tpu_custom_call" | custom-call | tf_op jit(solution)/shard_map/attention_block/pallas_call | solution.py:717
  141.8 1.8 %copy.16 = bf16[384,512]{1,0:T(8,128)(2,1)} copy(bf16[384,512]{1,0:T(8,128)(2,1)} %attention_block.1) | data formatting | bytes 786432

commit v6 on v5

--- a/solution.py
+++ b/solution.py
@@ -440,18 +440,6 @@
     kv_slot = weights.at[c, :, pl.ds(q_cols, HD)]
     key_copy = pltpu.make_async_copy(w_key.at[:, head_cols], kv_slot, local_sem.at[5])
     value_copy = pltpu.make_async_copy(w_value.at[:, head_cols], kv_slot, local_sem.at[5])
-    labels[...] = jnp.zeros_like(labels)
-    for copy in local + marks_here:
-        copy.start()
-
-    @pl.when(xl == 0)
-    def _():
-        key_copy.start()
-
-    @pl.when(xl == 1)
-    def _():
-        value_copy.start()
-
     links = neighbours()
     later = {}
     for ahead in (1, 2):
@@ -468,6 +456,18 @@
     barrier = pltpu.get_barrier_semaphore()
     for device in peers:
         pl.semaphore_signal(barrier, inc=1, device_id=device, device_id_type=MESH)
+
+    labels[...] = jnp.zeros_like(labels)
+    for copy in local + marks_here:
+        copy.start()
+
+    @pl.when(xl == 0)
+    def _():
+        key_copy.start()
+
+    @pl.when(xl == 1)
+    def _():
+        value_copy.start()
 
     @pl.when(core != xl)
     def _():

time: 144 us -> 144 us (level)
  no operation moved by 1% of the time
where the time goes in v6:
time: 144 us; the launch traced here: 143 us
  Pallas kernels  141 us (98%)
  local copies, waits for them, and re-layouts  1.77 us (1%)
    pallas_call x1, Pallas kernels, run_block(): pl.pallas_call(block_kernel, out_shape=jax.ShapeDtypeStruct((rows, cols),...  141 us

profile of v6, /device:TPU:4, one launch (start us, length us, event | category | flops | bytes accessed | tf_op | source)
XLA Modules:
  0.0 143.3 jit_solution(12618202236877687209)
XLA Ops:
  0.7 140.9 %attention_block.1 = bf16[384,512]{1,0:T(8,128)(2,1)} custom-call(bf16[384,512]{1,0:T(8,128)(2,1)} %stream.1, bf16[1,384,8192]{2,1,0:T(8,128)(2,1)} %pending.1, bf16[512,256]{1,0:T(8,128)(2,1)} %w_query.1, bf16[512,1024]{1,0:T(8,128)(2,1)} %w_key.1, bf16[512,1024]{1,0:T(8,128)(2,1)} %w_value.1, bf16[256,512]{1,0:T(8,128)(2,1)} %w_out.1, ...), custom_call_target="tpu_custom_call" | custom-call | tf_op jit(solution)/shard_map/attention_block/pallas_call | solution.py:717
  141.6 1.8 %copy.16 = bf16[384,512]{1,0:T(8,128)(2,1)} copy(bf16[384,512]{1,0:T(8,128)(2,1)} %attention_block.1) | data formatting | bytes 786432
